TPU v7x, 512 devices: a whole 4x8x8 slice. The times are simulated.
512 devices in a mesh: fsdp: 16 (over y, core), dp: 32 (over z, x).
Axes of the slice: x: 4, y: 8, z: 8, core: 2. Of those that a mesh axis runs over, the one named last changes fastest.
Arguments:
- acts: bfloat16 [32, 2048, 64], P('dp', 'fsdp'), may hold values from -6 to 6
- cot: bfloat16 [32, 2048, 14336], P('dp', 'fsdp'), may hold values from -0.125 to 0.125
- error_in: float32 [32, 64, 14336], P('dp', 'fsdp'), may hold values from -6 to 6
- q_warm: float32 [14336, 32], P('fsdp'), may hold values from -0.046875 to 0.046875
- quorum: int32 [32], replicated, may hold values from 0 to 1, as said below
- counts: int32 [32], replicated, may hold values from 1 to 4
Outputs:
- error_out: float32 [32, 64, 14336], P('dp', 'fsdp')
- approx: float32 [64, 14336], P('fsdp', 'dp')
- q_next: float32 [14336, 32], P('fsdp')
Inputs may be any that keep to these rules, and one draw needn't show every extreme that they name: At least one island has quorum 1.
All inputs are finite; a program needn't handle non-finite values.
Results may differ from a plain program's by a relative error of at most 0.0004.
Values sent between devices are 32-bit elements; how exact they have to be, the bound alone decides.
No kernel may reach another device: no remote copies, remote signals or barrier semaphores. Data moves between devices by JAX's collectives and lax.ppermute only.
A program may use at most 64 MiB of HBM per device.

v0:
```python
import jax
import jax.numpy as jnp
from jax import lax
from jax.sharding import PartitionSpec as P


def shards(acts, cot, error_in, q_warm, quorum, counts):
    highest = lax.Precision.HIGHEST
    inputs = acts[0]
    grads_out = cot[0]
    groups = lax.axis_size("fsdp")
    islands_axis = lax.axis_size("dp")
    partial_value = jnp.einsum("td,tf->df", inputs, grads_out, preferred_element_type=jnp.float32)
    share = lax.psum_scatter(partial_value, "fsdp", scatter_dimension=0, tiled=True)
    merged = share + error_in[0]
    whole_q = lax.all_gather(q_warm, "fsdp", axis=0, tiled=True)
    weight = (quorum * counts).astype(jnp.float32)
    total = jnp.sum(weight)
    islands = weight.shape[0]
    mine = jnp.sum(jnp.where(jnp.arange(islands) == lax.axis_index("dp"), weight, 0.0))
    local_p = jnp.dot(merged, whole_q, precision=highest) * mine
    p_sum = lax.psum(local_p, "dp") / total
    gram = lax.psum(jnp.dot(p_sum.T, p_sum, precision=highest), "fsdp")
    lower = jnp.linalg.cholesky(gram)
    p_hat = jax.scipy.linalg.solve_triangular(lower, p_sum.T, lower=True).T
    local_q = jnp.einsum("df,dr->fr", merged, p_hat, precision=highest) * mine
    q_whole = lax.psum(local_q, ("fsdp", "dp")) / total
    approx_full = jnp.dot(p_hat, q_whole.T, precision=highest)
    error_out = (merged - approx_full)[None]
    q_rows = q_whole.shape[0] // groups
    q_next = lax.dynamic_slice_in_dim(q_whole, lax.axis_index("fsdp") * q_rows, q_rows, 0)
    own_cols = approx_full.shape[1] // islands_axis
    approx = lax.dynamic_slice_in_dim(approx_full, lax.axis_index("dp") * own_cols, own_cols, 1)
    return (error_out, approx, q_next)


def solution(mesh):
    return jax.shard_map(
        shards,
        mesh=mesh,
        in_specs=(
            P("dp", "fsdp", None),
            P("dp", "fsdp", None),
            P("dp", "fsdp", None),
            P("fsdp", None),
            P(),
            P(),
        ),
        out_specs=(P("dp", "fsdp", None), P("fsdp", "dp"), P("fsdp", None)),
        check_vma=False,
    )
```

profile of v0, /device:TPU:1, one launch (start us, length us, event | category | flops | bytes accessed | tf_op | source)
XLA Modules:
  0.0 608.6 jit_solution(13223175797652288538)
XLA Ops:
  7.2 0.7 copy-done
  7.9 4.5 fusion
  12.5 0.7 all-gather.2.cloned.1.call-update
  13.2 1.3 dynamic-slice
  15.2 0.6 convert_reduce_fusion
  15.8 126.9 %all-reduce.6.cloned.1.call-done = f32[64,14336]{1,0:T(8,128)} async-done(((f32[64,14336]{1,0:T(8,128)}), f32[64,14336]{1,0:T(8,128)}) %all-reduce.6.cloned.1.call-update) | async-done | bytes 3670032
  142.7 1.1 dynamic-slice_add_fusion
  143.8 44.3 %all-gather.2.cloned.1.call-done = f32[14336,32]{0,1:T(8,128)} async-done(((f32[896,32]{0,1:T(8,128)}), f32[14336,32]{0,1:T(8,128)}) %all-gather.2.cloned.1.call-update) | async-done | bytes 1835024 | tf_op jit(solution)/shard_map/all_gather | solution.py:16
  188.0 3.7 convolution_multiply_fusion.1
  191.7 61.9 %psum.21 = f32[4,32]{1,0:T(4,128)S(1)} all-reduce(f32[4,32]{1,0:T(4,128)S(1)} %convolution_multiply_fusion.1), channel_id=1, replica_groups=mesh['fsdp'=16,'dp'=32] {'dp'}, use_global_device_ids=true, to_apply=%region_2.3 | all-reduce | flops 128 | bytes 1024 | tf_op jit(solution)/shard_map/psum | solution.py:22
  253.5 0.9 fusion.8
  254.4 56.3 %psum.22 = f32[32,32]{0,1:T(8,128)S(1)} all-reduce(f32[32,32]{0,1:T(8,128)S(1)} %fusion.8), channel_id=1, replica_groups=mesh['fsdp'=16,'dp'=32] {'fsdp'}, use_global_device_ids=true, to_apply=%region_4.5 | all-reduce | flops 1024 | bytes 8192 | tf_op jit(solution)/shard_map/psum | solution.py:23
  310.8 2.9 cholesky.16
  313.7 0.6 compare_reduce_fusion
  314.4 0.7 fusion.2
  315.0 2.4 custom-call.7
  317.4 0.8 fusion.3
  318.2 3.5 convolution_multiply_fusion
  321.8 274.9 %all-reduce.4.cloned.1.call-done = f32[14336,32]{0,1:T(8,128)} async-done(((f32[14336,32]{0,1:T(8,128)}), f32[14336,32]{0,1:T(8,128)}) %all-reduce.4.cloned.1.call-update) | async-done | bytes 1835024 | tf_op jit(solution)/shard_map/psum | solution.py:27
  596.7 2.3 broadcast_divide_fusion
  599.0 1.0 fusion.9
  600.0 0.7 subtract_bitcast_fusion
  600.7 0.7 constant_dynamic-slice_fusion.1
  601.4 0.7 constant_dynamic-slice_fusion
  (15 shorter events, 0.3 us)
Async XLA Ops:
  7.2 0.7 copy-start
  7.2 135.5 %all-reduce.6.cloned.1.call-start = ((), (), s32[]{:S(2)}) async-start(), calls=%async_computation.2 | async-start | bytes 7340032
  12.4 2.8 copy-start.2
  12.4 2.8 copy-start.3
  12.4 130.3 %copy-start.1 = (f32[1,4,14336]{2,1,0:T(4,128)S(1)}, f32[1,4,14336]{2,1,0:T(4,128)}, u32[]{:S(2)}) copy-start(f32[1,4,14336]{2,1,0:T(4,128)} %param.8) | copy-start | bytes 688132
  12.4 175.6 %all-gather.2.cloned.1.call-start = ((), (), s32[]{:S(2)}) async-start(), calls=%async_computation | async-start | bytes 1949696 | tf_op jit(solution)/shard_map/all_gather | solution.py:16
  13.2 583.5 %all-reduce.4.cloned.1.call-start = ((), (), s32[]{:S(2)}) async-start(), calls=%async_computation.1 | async-start | bytes 3670016 | tf_op jit(solution)/shard_map/psum | solution.py:27
Sparse Core Ops, SparseCore 0:
  12.5 130.0 all-reduce.5
  144.8 43.1 all-gather.1
  321.9 274.7 all-reduce.3
where the time goes:
time: 609 us
  waiting for transfers between devices  447 us (73%)
  blocking collectives  118 us (19%)
  between operations  14.5 us (2%)
  matrix products  14.3 us (2%)
  other arithmetic  11.4 us (2%)
    psum x1, waiting for transfers between devices, shards(): q_whole = lax.psum(local_q, ('fsdp', 'dp')) / total  275 us
    unnamed x4, waiting for transfers between devices  128 us
    psum x1, blocking collectives, shards(): p_sum = lax.psum(local_p, 'dp') / total  61.9 us
    psum x1, blocking collectives, shards(): gram = lax.psum(jnp.dot(p_sum.T, p_sum, precision=highest), 'fsdp')  56.3 us
    all_gather x1, waiting for transfers between devices, shards(): whole_q = lax.all_gather(q_warm, 'fsdp', axis=0, tiled=True)  44.3 us
  transfers between devices with their start and end apart: 3, of which 3 were waited for; matrix products, arithmetic and copies ran while one was open for 0% of the time, Pallas kernels for 0%

commit v1 on v0

v1 whole, which is shorter than its diff:
```python
import jax
import jax.numpy as jnp
from jax import lax
from jax.sharding import PartitionSpec as P

HIGHEST = lax.Precision.HIGHEST


def shards(acts, cot, error_in, q_warm, quorum, counts):
    groups = lax.axis_size("fsdp")
    islands = lax.axis_size("dp")
    chips = groups // 2
    f = lax.axis_index("fsdp")
    i = lax.axis_index("dp")
    y, core = f // 2, f % 2
    a, c = acts[0], cot[0]
    rank = q_warm.shape[1]
    d_blk, f_blk = a.shape[1], c.shape[1]
    rows = d_blk // groups
    chunk = 2 * rows
    half = chips // 2
    cols = f_blk // islands
    piece = f_blk // (groups * islands)

    whole_q = lax.all_gather(q_warm, "fsdp", axis=0, tiled=True)

    weight = (quorum * counts).astype(jnp.float32)
    total = jnp.sum(weight)
    mine = jnp.sum(jnp.where(jnp.arange(islands) == i, weight, 0.0)) / total

    up = [y + d for d in range(half - 1, 0, -1)] + [y + half]
    down = [y - d for d in range(half - 1, 0, -1)] + [y]
    order = jnp.where(core == 0, jnp.stack(up + down), jnp.stack(down + up)) % chips
    picked = (order[:, None] * chunk + jnp.arange(chunk)[None, :]).reshape(-1)
    onehot = (picked[None, :] == jnp.arange(d_blk)[:, None]).astype(a.dtype)
    chosen = jnp.dot(a, onehot, preferred_element_type=jnp.float32).astype(a.dtype)
    other = jnp.einsum("td,tf->df", chosen[:, d_blk // 2 :], c, preferred_element_type=jnp.float32)
    swap = [(k, k ^ 1) for k in range(groups)]
    got = lax.ppermute(other, "fsdp", swap)
    own = jnp.einsum("td,tf->df", chosen[:, : d_blk // 2], c, preferred_element_type=jnp.float32)
    both = (own + got).reshape(half, chunk, f_blk)

    ring = [(2 * k, 2 * ((k + 1) % chips)) for k in range(chips)] + [(2 * k + 1, 2 * ((k - 1) % chips) + 1) for k in range(chips)]
    run = lax.ppermute(both[half - 1], "fsdp", ring)
    run = jnp.where(core == 0, run, 0.0)
    for k in range(half - 1):
        run = lax.ppermute(run + both[k], "fsdp", ring)
    run = run + jnp.where(core == 1, both[half - 1], 0.0)
    share = run + lax.ppermute(run, "fsdp", swap)
    share = lax.dynamic_slice_in_dim(share, core * rows, rows, 0)
    merged = share + error_in[0]

    p_rows = jnp.dot(merged, whole_q, precision=HIGHEST)
    sent = merged.reshape(rows, islands, cols).transpose(1, 0, 2)
    sent = jnp.concatenate([sent, jnp.broadcast_to(p_rows[None], (islands, rows, rank))], axis=2) * mine
    mean_rows = jnp.sum(lax.all_to_all(sent, "dp", 0, 0, tiled=True), axis=0)
    width = cols + rank
    sent = jnp.broadcast_to(mean_rows[None], (groups, rows, width))
    mean = lax.all_to_all(sent, "fsdp", 0, 0, tiled=True).reshape(d_blk, width)
    mean_m, p_sum = mean[:, :cols], mean[:, cols:]

    part = islands // 2
    moves = []
    for g in range(groups):
        for k in range(islands):
            moves.append((g * islands + k, (k // 2) * islands + (k % 2) * part + g))
    m_piece = lax.dynamic_slice_in_dim(mean_m, f * piece, piece, 1)
    m_piece = lax.ppermute(m_piece, ("fsdp", "dp"), moves)

    gram = jnp.dot(p_sum.T, p_sum, precision=HIGHEST)
    lower = jnp.linalg.cholesky(gram)
    p_hat = jax.scipy.linalg.solve_triangular(lower, p_sum.T, lower=True).T

    q_cols = jnp.dot(p_hat.T, mean_m, precision=HIGHEST)
    p_own = lax.dynamic_slice_in_dim(p_hat, f * rows, rows, 0)
    approx = jnp.dot(p_own, q_cols, precision=HIGHEST)
    q_piece = jnp.dot(p_hat.T, m_piece, precision=HIGHEST)
    extra = rank * piece // rows
    sent = jnp.concatenate([approx, q_piece.reshape(rows, extra)], axis=1)
    sent = jnp.broadcast_to(sent[None], (islands, rows, cols + extra))
    got = lax.all_to_all(sent, "dp", 0, 0, tiled=True)
    approx_rows = got[:, :, :cols].transpose(1, 0, 2).reshape(rows, f_blk)
    q_next = got[:, :, cols:].reshape(islands, rank, piece).transpose(0, 2, 1).reshape(islands * piece, rank)
    error_out = (merged - approx_rows)[None]
    return (error_out, approx, q_next)


def solution(mesh):
    return jax.shard_map(
        shards,
        mesh=mesh,
        in_specs=(
            P("dp", "fsdp", None),
            P("dp", "fsdp", None),
            P("dp", "fsdp", None),
            P("fsdp", None),
            P(),
            P(),
        ),
        out_specs=(P("dp", "fsdp", None), P("fsdp", "dp"), P("fsdp", None)),
        check_vma=False,
    )
```

time: 609 us -> 204 us (0.33)
  waiting for transfers between devices: 447 us -> 80.9 us
  blocking collectives: 118 us -> 45.3 us
  starting transfers between devices: 0.12 us -> 41.1 us
  matrix products: 14.3 us -> 7.79 us
    psum x1 -> x0, waiting for transfers between devices: 275 us -> none  [shards(): q_whole = lax.psum(local_q, ('fsdp', 'dp')) / total]
    unnamed x4 -> x1, waiting for transfers between devices: 128 us -> 0.02 us
    psum x2 -> x0, blocking collectives: 118 us -> none  [the longest x1 61.9 us: shards(): p_sum = lax.psum(local_p, 'dp') / total]
    all_to_all x0 -> x2, blocking collectives: none -> 45.3 us  [the longest x1 23.9 us: shards(): got = lax.all_to_all(sent, 'dp', 0, 0, tiled=True)]
    ppermute x0 -> x7, starting transfers between devices: none -> 34.3 us  [the longest x3 11.7 us: shards(): run = lax.ppermute(run + both[k], 'fsdp', ring)]
    ppermute x0 -> x7, waiting for transfers between devices: none -> 33.1 us  [the longest x3 17.5 us: shards(): run = lax.ppermute(run + both[k], 'fsdp', ring)]
    all_to_all x0 -> x1, waiting for transfers between devices: none -> 9.17 us  [shards(): mean = lax.all_to_all(sent, 'fsdp', 0, 0, tiled=True).reshape(d_blk, width)]
    all_to_all x0 -> x1, starting transfers between devices: none -> 6.82 us  [shards(): mean = lax.all_to_all(sent, 'fsdp', 0, 0, tiled=True).reshape(d_blk, width)]
  transfers between devices with their start and end apart: 3 -> 9, of which waited for: 3 -> 8; matrix products, arithmetic and copies ran while one was open for 0% -> 1% of each run, Pallas kernels for 0% -> 0%
where the time goes in v1:
time: 204 us; the launch traced here: 203 us
  waiting for transfers between devices  80.9 us (40%)
  blocking collectives  45.3 us (22%)
  starting transfers between devices  41.1 us (20%)
  between operations  15.7 us (8%)
  other arithmetic  8.73 us (4%)
  matrix products  7.79 us (4%)
  local copies, waits for them, and re-layouts  3.87 us (2%)
    all_gather x1, waiting for transfers between devices, shards(): whole_q = lax.all_gather(q_warm, 'fsdp', axis=0, tiled=True)  38.6 us
    all_to_all x1, blocking collectives, shards(): got = lax.all_to_all(sent, 'dp', 0, 0, tiled=True)  23.9 us
    all_to_all x1, blocking collectives, shards(): mean_rows = jnp.sum(lax.all_to_all(sent, 'dp', 0, 0, tiled=True), axis=0)  21.4 us
    ppermute x3, waiting for transfers between devices, shards(): run = lax.ppermute(run + both[k], 'fsdp', ring)  17.5 us
    ppermute x3, starting transfers between devices, shards(): run = lax.ppermute(run + both[k], 'fsdp', ring)  11.7 us
    ppermute x1, starting transfers between devices, shards(): share = run + lax.ppermute(run, 'fsdp', swap)  9.98 us
    all_to_all x1, waiting for transfers between devices, shards(): mean = lax.all_to_all(sent, 'fsdp', 0, 0, tiled=True).reshape(d_blk, width)  9.17 us
    ppermute x1, starting transfers between devices, shards(): got = lax.ppermute(other, 'fsdp', swap)  8.79 us
  transfers between devices with their start and end apart: 9, of which 8 were waited for; matrix products, arithmetic and copies ran while one was open for 1% of the time, Pallas kernels for 0%

profile of v1, /device:TPU:1, one launch (start us, length us, event | category | flops | bytes accessed | tf_op | source)
XLA Modules:
  0.0 203.4 jit_solution(587397314439219778)
XLA Ops:
  8.1 2.8 %fusion = f32[32,14336]{1,0:T(8,128)S(1)} fusion(bf16[1,128,14336]{2,1,0:T(8,128)(2,1)} %param.7, bf16[128,64]{0,1:T(8,128)(2,1)S(1)} %fusion.3), kind=kOutput, calls=%fused_computation.1 | convolution fusion | flops 117440512 | bytes 5513216 | tf_op jit(solution)/shard_map/td,tf->df/dot_general | solution.py:37
  10.9 8.8 %collective-permute-start = (f32[32,14336]{1,0:T(8,128)S(1)}, f32[32,14336]{1,0:T(8,128)S(1)}, u32[]{:S(2)}, u32[]{:S(2)}) collective-permute-start(f32[32,14336]{1,0:T(8,128)S(1)} %fusion), channel_id=1, source_target_pairs={{0,32},{32,0},{64,96},{96,64},{128,160},{160,128},{192,224},{224,1... | collective-permute-start | bytes 5505032 | tf_op jit(solution)/shard_map/ppermute | solution.py:39
  19.7 3.4 %collective-permute-done = f32[32,14336]{1,0:T(8,128)S(1)} collective-permute-done((f32[32,14336]{1,0:T(8,128)S(1)}, f32[32,14336]{1,0:T(8,128)S(1)}, u32[]{:S(2)}, u32[]{:S(2)}) %collective-permute-start) | collective-permute-done | bytes 1835040 | tf_op jit(solution)/shard_map/ppermute | solution.py:39
  23.7 1.9 collective-permute-start.1
  25.7 7.6 %collective-permute-done.1 = f32[8,14336]{1,0:T(8,128)S(1)} collective-permute-done((f32[8,14336]{1,0:T(8,128)S(1)}, f32[8,14336]{1,0:T(8,128)S(1)}, u32[]{:S(2)}, u32[]{:S(2)}) %collective-permute-start.1) | collective-permute-done | bytes 458784 | tf_op jit(solution)/shard_map/ppermute | solution.py:44
  33.3 3.0 %collective-permute-start.2 = (f32[8,14336]{1,0:T(8,128)S(1)}, f32[8,14336]{1,0:T(8,128)S(1)}, u32[]{:S(2)}, u32[]{:S(2)}) collective-permute-start(f32[8,14336]{1,0:T(8,128)S(1)} %slice_add_fusion.2), channel_id=1, source_target_pairs={{0,64},{64,128},{128,192},{192,256},{256,320},{320,384},{384,448},... | collective-permute-start | bytes 1376264 | tf_op jit(solution)/shard_map/ppermute | solution.py:47
  36.3 6.7 %collective-permute-done.2 = f32[8,14336]{1,0:T(8,128)S(1)} collective-permute-done((f32[8,14336]{1,0:T(8,128)S(1)}, f32[8,14336]{1,0:T(8,128)S(1)}, u32[]{:S(2)}, u32[]{:S(2)}) %collective-permute-start.2) | collective-permute-done | bytes 458784 | tf_op jit(solution)/shard_map/ppermute | solution.py:47
  43.1 3.8 %collective-permute-start.3 = (f32[8,14336]{1,0:T(8,128)S(1)}, f32[8,14336]{1,0:T(8,128)S(1)}, u32[]{:S(2)}, u32[]{:S(2)}) collective-permute-start(f32[8,14336]{1,0:T(8,128)S(1)} %slice_add_fusion.1), channel_id=1, source_target_pairs={{0,64},{64,128},{128,192},{192,256},{256,320},{320,384},{384,448},... | collective-permute-start | bytes 1376264 | tf_op jit(solution)/shard_map/ppermute | solution.py:47
  46.8 5.5 %collective-permute-done.3 = f32[8,14336]{1,0:T(8,128)S(1)} collective-permute-done((f32[8,14336]{1,0:T(8,128)S(1)}, f32[8,14336]{1,0:T(8,128)S(1)}, u32[]{:S(2)}, u32[]{:S(2)}) %collective-permute-start.3) | collective-permute-done | bytes 458784 | tf_op jit(solution)/shard_map/ppermute | solution.py:47
  52.4 5.0 %collective-permute-start.4 = (f32[8,14336]{1,0:T(8,128)S(1)}, f32[8,14336]{1,0:T(8,128)S(1)}, u32[]{:S(2)}, u32[]{:S(2)}) collective-permute-start(f32[8,14336]{1,0:T(8,128)S(1)} %slice_add_fusion), channel_id=1, source_target_pairs={{0,64},{64,128},{128,192},{192,256},{256,320},{320,384},{384,448},... | collective-permute-start | bytes 1376264 | tf_op jit(solution)/shard_map/ppermute | solution.py:47
  57.3 5.4 %collective-permute-done.4 = f32[8,14336]{1,0:T(8,128)S(1)} collective-permute-done((f32[8,14336]{1,0:T(8,128)S(1)}, f32[8,14336]{1,0:T(8,128)S(1)}, u32[]{:S(2)}, u32[]{:S(2)}) %collective-permute-start.4) | collective-permute-done | bytes 458784 | tf_op jit(solution)/shard_map/ppermute | solution.py:47
  62.8 10.0 %collective-permute-start.5 = (f32[8,14336]{1,0:T(8,128)S(1)}, f32[8,14336]{1,0:T(8,128)S(1)}, u32[]{:S(2)}, u32[]{:S(2)}) collective-permute-start(f32[8,14336]{1,0:T(8,128)S(1)} %select_add_fusion), channel_id=1, source_target_pairs={{0,32},{32,0},{64,96},{96,64},{128,160},{160,128},{192,224},{224,1... | collective-permute-start | bytes 1376264 | tf_op jit(solution)/shard_map/ppermute | solution.py:49
  75.2 38.6 %all-gather.2.cloned.1.call-done = f32[14336,32]{0,1:T(8,128)} async-done(((f32[896,32]{0,1:T(8,128)}), f32[14336,32]{0,1:T(8,128)}) %all-gather.2.cloned.1.call-update) | async-done | bytes 1835024 | tf_op jit(solution)/shard_map/all_gather | solution.py:25
  113.8 3.0 %fusion.24 = f32[4,32]{1,0:T(4,128)S(1)} fusion(f32[4,14336]{1,0:T(4,128)S(1)} %fusion.4, f32[14336,32]{0,1:T(8,128)} %all-gather.2.cloned.1.call-done), kind=kOutput, calls=%fused_computation.51 | convolution fusion | flops 22020096 | bytes 2064896 | tf_op jit(solution)/shard_map/dot_general | solution.py:53
  117.0 21.4 %all_to_all.15 = f32[32,4,480]{2,1,0:T(4,128)S(1)} all-to-all(f32[32,4,480]{2,1,0:T(4,128)S(1)} %maximum_multiply_fusion), channel_id=1, replica_groups=mesh['fsdp'=16,'dp'=32] {'dp'}, dimensions={0} | all-to-all | bytes 491520 | tf_op jit(solution)/shard_map/all_to_all | solution.py:56
  139.1 6.8 %all-to-all-start.1 = ((f32[16,4,480]{2,1,0:T(4,128)}), f32[16,4,480]{2,1,0:T(4,128)S(1)}, u32[]{:S(2)}, u32[]{:S(2)}) async-start(f32[16,4,480]{2,1,0:T(4,128)} %broadcast_in_dim.38), calls=%async_computation.1 | async-start | bytes 262144 | tf_op jit(solution)/shard_map/all_to_all | solution.py:59
  145.9 9.2 %all-to-all-done.1 = f32[16,4,480]{2,1,0:T(4,128)S(1)} async-done(((f32[16,4,480]{2,1,0:T(4,128)}), f32[16,4,480]{2,1,0:T(4,128)S(1)}, u32[]{:S(2)}, u32[]{:S(2)}) %all-to-all-start.1) | async-done | bytes 122912 | tf_op jit(solution)/shard_map/all_to_all | solution.py:59
  155.5 2.9 %cholesky.16 = f32[32,32]{1,0:T(8,128)S(1)} custom-call(f32[32,32]{1,0:T(8,128)S(1)} %fusion.11), custom_call_target="Cholesky" | custom-call | tf_op jit(solution)/shard_map/jit(cholesky)/cholesky | solution.py:71
  159.8 2.4 %custom-call.7 = f32[1,32,32]{1,2,0:T(8,128)S(1)} custom-call(f32[1,32,32]{2,1,0:T(8,128)S(1)} %fusion.9), custom_call_target="InvertDiagBlocksLowerTriangular" | custom-call | tf_op jit(solution)/shard_map/jit(_solve_triangular)/triangular_solve | solution.py:72
  162.8 1.9 collective-permute-start.6
  165.0 4.6 %collective-permute-done.6 = f32[64,28]{1,0:T(8,128)S(1)} collective-permute-done((f32[64,28]{1,0:T(8,128)S(1)}, f32[64,28]{1,0:T(8,128)S(1)}, u32[]{:S(2)}, u32[]{:S(2)}) %collective-permute-start.6) | collective-permute-done | bytes 7200 | tf_op jit(solution)/shard_map/ppermute | solution.py:68
  170.0 23.9 %all_to_all.16 = f32[32,4,672]{2,1,0:T(4,128)S(1)} all-to-all(f32[32,4,672]{2,1,0:T(4,128)S(1)} %broadcast_in_dim.39), channel_id=1, replica_groups=mesh['fsdp'=16,'dp'=32] {'dp'}, dimensions={0} | all-to-all | bytes 688128 | tf_op jit(solution)/shard_map/all_to_all | solution.py:81
  194.6 0.9 reshape.207
  195.8 0.8 subtract_bitcast_fusion
  (56 shorter events, 7.6 us)
Async XLA Ops:
  7.2 0.7 copy-start
  7.2 106.7 %all-gather.2.cloned.1.call-start = ((), (), s32[]{:S(2)}) async-start(), calls=%async_computation.3 | async-start | bytes 1949696 | tf_op jit(solution)/shard_map/all_gather | solution.py:25
  8.1 15.0 %copy-start.1 = (bf16[1,128,14336]{2,1,0:T(8,128)(2,1)S(1)}, bf16[1,128,14336]{2,1,0:T(8,128)(2,1)}, u32[]{:S(2)}) copy-start(bf16[1,128,14336]{2,1,0:T(8,128)(2,1)} %param.7) | copy-start | bytes 11010052
  10.9 12.2 %collective-permute-start = (f32[32,14336]{1,0:T(8,128)S(1)}, f32[32,14336]{1,0:T(8,128)S(1)}, u32[]{:S(2)}, u32[]{:S(2)}) collective-permute-start(f32[32,14336]{1,0:T(8,128)S(1)} %fusion), channel_id=1, source_target_pairs={{0,32},{32,0},{64,96},{96,64},{128,160},{160,128},{192,224},{224,1... | collective-permute-start | bytes 5505032 | tf_op jit(solution)/shard_map/ppermute | solution.py:39
  23.7 9.5 %collective-permute-start.1 = (f32[8,14336]{1,0:T(8,128)S(1)}, f32[8,14336]{1,0:T(8,128)S(1)}, u32[]{:S(2)}, u32[]{:S(2)}) collective-permute-start(f32[8,14336]{1,0:T(8,128)S(1)} %slice.59), channel_id=1, source_target_pairs={{0,64},{64,128},{128,192},{192,256},{256,320},{320,384},{384,448},... | collective-permute-start | bytes 1376264 | tf_op jit(solution)/shard_map/ppermute | solution.py:44
  33.3 39.5 %copy-start.4 = (s32[32]{0:T(128)S(1)}, s32[32]{0:T(128)}, u32[]{:S(2)}) copy-start(s32[32]{0:T(128)} %param.10) | copy-start | bytes 388
  33.3 39.5 %copy-start.5 = (s32[32]{0:T(128)S(1)}, s32[32]{0:T(128)}, u32[]{:S(2)}) copy-start(s32[32]{0:T(128)} %param.11) | copy-start | bytes 388
  33.3 41.5 %copy-start.2 = (f32[1,4,14336]{2,1,0:T(4,128)S(1)}, f32[1,4,14336]{2,1,0:T(4,128)}, u32[]{:S(2)}) copy-start(f32[1,4,14336]{2,1,0:T(4,128)} %param.8) | copy-start | bytes 688132
  33.3 9.6 %collective-permute-start.2 = (f32[8,14336]{1,0:T(8,128)S(1)}, f32[8,14336]{1,0:T(8,128)S(1)}, u32[]{:S(2)}, u32[]{:S(2)}) collective-permute-start(f32[8,14336]{1,0:T(8,128)S(1)} %slice_add_fusion.2), channel_id=1, source_target_pairs={{0,64},{64,128},{128,192},{192,256},{256,320},{320,384},{384,448},... | collective-permute-start | bytes 1376264 | tf_op jit(solution)/shard_map/ppermute | solution.py:47
  43.1 9.2 %collective-permute-start.3 = (f32[8,14336]{1,0:T(8,128)S(1)}, f32[8,14336]{1,0:T(8,128)S(1)}, u32[]{:S(2)}, u32[]{:S(2)}) collective-permute-start(f32[8,14336]{1,0:T(8,128)S(1)} %slice_add_fusion.1), channel_id=1, source_target_pairs={{0,64},{64,128},{128,192},{192,256},{256,320},{320,384},{384,448},... | collective-permute-start | bytes 1376264 | tf_op jit(solution)/shard_map/ppermute | solution.py:47
  52.4 10.4 %collective-permute-start.4 = (f32[8,14336]{1,0:T(8,128)S(1)}, f32[8,14336]{1,0:T(8,128)S(1)}, u32[]{:S(2)}, u32[]{:S(2)}) collective-permute-start(f32[8,14336]{1,0:T(8,128)S(1)} %slice_add_fusion), channel_id=1, source_target_pairs={{0,64},{64,128},{128,192},{192,256},{256,320},{320,384},{384,448},... | collective-permute-start | bytes 1376264 | tf_op jit(solution)/shard_map/ppermute | solution.py:47
  62.8 12.0 %collective-permute-start.5 = (f32[8,14336]{1,0:T(8,128)S(1)}, f32[8,14336]{1,0:T(8,128)S(1)}, u32[]{:S(2)}, u32[]{:S(2)}) collective-permute-start(f32[8,14336]{1,0:T(8,128)S(1)} %select_add_fusion), channel_id=1, source_target_pairs={{0,32},{32,0},{64,96},{96,64},{128,160},{160,128},{192,224},{224,1... | collective-permute-start | bytes 1376264 | tf_op jit(solution)/shard_map/ppermute | solution.py:49
  139.1 16.0 %all-to-all-start.1 = ((f32[16,4,480]{2,1,0:T(4,128)}), f32[16,4,480]{2,1,0:T(4,128)S(1)}, u32[]{:S(2)}, u32[]{:S(2)}) async-start(f32[16,4,480]{2,1,0:T(4,128)} %broadcast_in_dim.38), calls=%async_computation.1 | async-start | bytes 262144 | tf_op jit(solution)/shard_map/all_to_all | solution.py:59
  162.8 6.8 %collective-permute-start.6 = (f32[64,28]{1,0:T(8,128)S(1)}, f32[64,28]{1,0:T(8,128)S(1)}, u32[]{:S(2)}, u32[]{:S(2)}) collective-permute-start(f32[64,28]{1,0:T(8,128)S(1)} %constant_dynamic-slice_fusion), channel_id=1, source_target_pairs={{0,0},{1,16},{2,32},{3,48},{4,64},{5,80},{6,96},{7,112},{8,128},{9... | collective-permute-start | bytes 21512 | tf_op jit(solution)/shard_map/ppermute | solution.py:68
  165.0 30.5 %copy-start.3 = (f32[4,448]{1,0:T(4,128)}, f32[4,448]{1,0:T(4,128)S(1)}, u32[]{:S(2)}) copy-start(f32[4,448]{1,0:T(4,128)S(1)} %fusion.13) | copy-start | bytes 21508
Sparse Core Ops, SparseCore 0:
  72.9 40.8 all-gather.1

commit v2 on v0

v2 whole, which is shorter than its diff:
```python
import functools

import jax
import jax.numpy as jnp
from jax import lax
from jax.experimental import pallas as pl
from jax.experimental.pallas import tpu as pltpu
from jax.sharding import PartitionSpec as P

HIGHEST = lax.Precision.HIGHEST
LANES = 128
SLOT = 32
F32 = jnp.float32


def iota(shape, axis):
    return lax.broadcasted_iota(jnp.int32, shape, axis)


def contract(x, z, dims):
    return lax.dot_general(x, z, ((dims[:1], dims[1:]), ((), ())), precision=HIGHEST, preferred_element_type=F32)


def pack_kernel(n_dp, piece, where_ref, mine_ref, own_ref, got_ref, q_ref, *refs):
    *shard_refs, sent_ref, merged_ref, chip_ref = refs
    y, core = where_ref[0], where_ref[1]
    chips, span = len(shard_refs) + 1, q_ref.shape[1]
    mid = merged_ref.shape[1]
    chip_ref[...] = own_ref[...] + got_ref[...]

    rank = q_ref.shape[0]
    parts = jnp.zeros((8, rank), F32)
    for k in range(chips):
        if k == 0:
            shard, chip = q_ref[...], y
        else:
            held = shard_refs[k - 1][...]
            shard = jnp.concatenate([held[:, a * span : (a + 1) * span] for a in range(rank // 8)], axis=0)
            step = k if k <= chips // 2 else k - chips // 2
            back = (core == 0) if k <= chips // 2 else (core == 1)
            chip = lax.rem(y + jnp.where(back, chips - step, step), chips)
        start = pl.multiple_of((2 * chip + core) * span, LANES)
        parts = parts + contract(chip_ref[:, pl.ds(start, span)], shard, (1, 1))

    left, right = chip_ref[:, :mid], chip_ref[:, mid:]
    low = iota((8, mid), 0) < 4
    upper = jnp.where(low, left, pltpu.roll(right, 4, 0))
    lower = jnp.where(low, pltpu.roll(left, 4, 0), right)
    merged = jnp.where(core == 0, upper, lower)
    merged_ref[...] = merged
    mine = mine_ref[0]
    scaled = merged * mine

    slots = mid // span
    width = slots * SLOT
    spot = (iota((rank, width), 1) // SLOT) * (SLOT - piece) + iota((rank, width), 1) % SLOT - piece
    place = ((iota((rank, width), 1) % SLOT >= piece) & (spot == iota((rank, width), 0))).astype(F32)
    base = contract(parts * mine, place, (1, 0))
    lane = iota((8, LANES), 1)
    for k in range(n_dp):
        first = (k * piece) // LANES
        for v in range(width // LANES):
            out = base[:, v * LANES : (v + 1) * LANES]
            for b in range(LANES // SLOT):
                f = v * (LANES // SLOT) + b
                for w in range(first, (k * piece + piece - 1) // LANES + 1):
                    src = f * span + w * LANES
                    at = k * piece - w * LANES
                    moved = pltpu.roll(scaled[:, src : src + LANES], (b * SLOT - at) % LANES, 1)
                    lo = b * SLOT + max(0, -at)
                    hi = b * SLOT + min(piece, LANES - at)
                    out = jnp.where((lane >= lo) & (lane < hi), moved, out)
            sent_ref[k, :, v * LANES : (v + 1) * LANES] = out


def factor_kernel(piece, where_ref, mean_ref, sent_ref):
    f = where_ref[0]
    groups, _, width = mean_ref.shape
    slots = width // SLOT
    rank = slots * (SLOT - piece)
    d_blk = groups * 4
    mean = mean_ref[...].reshape(groups * 8, width)
    lane_i, sub_i = iota((width, LANES), 0), iota((width, LANES), 1)
    pick = ((lane_i % SLOT >= piece) & ((lane_i // SLOT) * (SLOT - piece) + lane_i % SLOT - piece == sub_i)).astype(F32)
    p_all = contract(mean, pick, (1, 0)).reshape(groups // 2, 2, 8, LANES)
    p_sum = (p_all[:, 0] + p_all[:, 1]).reshape(d_blk, LANES)

    sub, lane = iota((d_blk, LANES), 0), iota((d_blk, LANES), 1)
    wide = p_sum + (lane == sub + rank).astype(F32)
    a = contract(p_sum, wide, (0, 0))[:rank]
    row_i = iota((rank, LANES), 0)
    for k in range(rank):
        pivot = a[k : k + 1, k : k + 1]
        inv = lax.rsqrt(pivot)
        inv = inv * (1.5 - 0.5 * pivot * inv * inv)
        row = a[k : k + 1, :] * inv
        col = jnp.where(row_i[:, :1] > k, a[:, k : k + 1] * inv, 0.0)
        a = jnp.where(row_i == k, row, a - col * row)

    approx = jnp.zeros((8, width), F32)
    halves = []
    src, dst = iota((LANES, groups * 8), 0) - rank, iota((LANES, groups * 8), 1)
    for h in range(2):
        spread = ((dst % 8 // 4 == h) & (src == dst // 8 * 4 + dst % 4)).astype(F32)
        q_half = contract(contract(a, spread, (1, 0)), mean, (1, 0))
        own = ((iota((LANES, 8), 1) // 4 == h) & (iota((LANES, 8), 0) - rank == f * 4 + iota((LANES, 8), 1) % 4)).astype(F32)
        approx = approx + contract(contract(a, own, (1, 0)), q_half, (0, 0))
        halves.append(q_half)
    q_mine = jnp.where(f < slots, halves[0], halves[1])
    q_mine = pltpu.roll(q_mine, lax.rem(width - lax.rem(f, slots) * SLOT, width), 1)[:, :LANES]
    lane = iota((8, LANES), 1)
    q_out = jnp.zeros((8, LANES), F32)
    for b in range(rank // 8):
        q_out = jnp.where(lane // SLOT == b, pltpu.roll(q_mine[b * 8 : b * 8 + 8], b * SLOT, 1), q_out)
    for k in range(sent_ref.shape[0]):
        sent_ref[k, :, :width] = approx
        sent_ref[k, :, width:] = q_out


def unpack_kernel(piece, where_ref, got_ref, merged_ref, error_ref, approx_ref, q_ref, whole_ref):
    i = where_ref[0]
    n_dp, _, width = got_ref.shape
    width -= LANES
    mid = merged_ref.shape[1]
    span = q_ref.shape[1]
    slots = width // SLOT
    lane = iota((8, LANES), 1)
    for f in range(slots):
        v, b = f * SLOT // LANES, f % (LANES // SLOT)
        for w in range(span // LANES):
            out = jnp.zeros((8, LANES), F32)
            for k in range(w * LANES // piece, ((w + 1) * LANES - 1) // piece + 1):
                at = k * piece - w * LANES
                moved = pltpu.roll(got_ref[k, :, v * LANES : (v + 1) * LANES], (at - b * SLOT) % LANES, 1)
                out = jnp.where((lane >= at) & (lane < at + piece), moved, out)
            whole_ref[:, f * span + w * LANES : f * span + (w + 1) * LANES] = out
    for b in range(q_ref.shape[0] // 8):
        for w in range(span // LANES):
            out = jnp.zeros((8, LANES), F32)
            for k in range(w * LANES // piece, ((w + 1) * LANES - 1) // piece + 1):
                at = k * piece - w * LANES
                moved = pltpu.roll(got_ref[k, :, width:], (at - b * SLOT) % LANES, 1)
                out = jnp.where((lane >= at) & (lane < at + piece), moved, out)
            q_ref[b * 8 : b * 8 + 8, w * LANES : (w + 1) * LANES] = out
    error = merged_ref[...] - whole_ref[...]
    error_ref[:, :mid] = error[:4]
    error_ref[:, mid:] = error[4:]
    cols = approx_ref.shape[1]
    per_half = mid // cols
    at = lax.rem(i, per_half) * cols
    start = pl.multiple_of(at // LANES * LANES, LANES)
    window = whole_ref[:, pl.ds(start, cols + LANES // 2)]
    window = jnp.where(lax.rem(at, LANES) == 0, window, pltpu.roll(window, cols, 1))
    window = jnp.where(i < per_half, window[:4], window[4:])
    approx_ref[...] = window[:, :cols]


VMEM = pl.BlockSpec(memory_space=pltpu.VMEM)
SMEM = pl.BlockSpec(memory_space=pltpu.SMEM)
PARAMS = pltpu.CompilerParams(vmem_limit_bytes=24 * 2**20)


def shards(acts, cot, error_in, q_warm, quorum, counts):
    groups = lax.axis_size("fsdp")
    islands = lax.axis_size("dp")
    chips = groups // 2
    f = lax.axis_index("fsdp")
    i = lax.axis_index("dp")
    y, core = f // 2, f % 2
    a, c = acts[0], cot[0]
    own_q, rank = q_warm.shape
    d_blk, f_blk = a.shape[1], c.shape[1]
    rows = d_blk // groups
    chunk = 2 * rows
    half = chips // 2
    cols = f_blk // islands
    piece = own_q // islands
    mid = f_blk // 2

    weight = (quorum * counts).astype(F32)
    total = jnp.sum(weight)
    mine = jnp.sum(jnp.where(jnp.arange(islands) == i, weight, 0.0)) / total

    up = [y + d for d in range(half - 1, 0, -1)] + [y + half]
    down = [y - d for d in range(half - 1, 0, -1)] + [y]
    order = jnp.where(core == 0, jnp.stack(up + down), jnp.stack(down + up)) % chips
    picked = (order[:, None] * chunk + jnp.arange(chunk)[None, :]).reshape(-1)
    onehot = (picked[None, :] == jnp.arange(d_blk)[:, None]).astype(a.dtype)
    chosen = jnp.dot(a, onehot, preferred_element_type=F32).astype(a.dtype)
    first, second = chosen[:, : d_blk // 2], chosen[:, d_blk // 2 :]

    def product(x, z):
        return jnp.einsum("td,tf->df", x, z, preferred_element_type=F32)

    swap = [(k, k ^ 1) for k in range(groups)]
    rise = [(2 * k, 2 * ((k + 1) % chips)) for k in range(chips)] + [(2 * k + 1, 2 * ((k - 1) % chips) + 1) for k in range(chips)]
    fall = [(2 * k, 2 * ((k - 1) % chips)) for k in range(chips)] + [(2 * k + 1, 2 * ((k + 1) % chips) + 1) for k in range(chips)]
    rings = (rise, fall)
    rising = (core == 0, core == 1)

    q_t = q_warm.T
    held = q_t.reshape(rank // 8, 8, own_q).transpose(1, 0, 2).reshape(8, rank // 8 * own_q)
    both, run, shards_q = [], [], [[], []]
    for x, other, z in ((first, second, c[:, :mid]), (second, first, c[:, mid:])):
        got = lax.ppermute(product(other, z), "fsdp", swap)
        both.append((product(x, z) + got).reshape(half, chunk, mid))
    run = [lax.ppermute(jnp.concatenate([both[s][half - 1], held], axis=1), "fsdp", rings[s]) for s in range(2)]
    for k in range(half):
        for s in range(2):
            if run[s].shape[1] > mid:
                shards_q[s].append(run[s][:, mid:])
                run[s] = run[s][:, :mid]
            if k == 0:
                run[s] = jnp.where(rising[s], run[s], 0.0)
        if k < half - 1:
            for s in range(2):
                nxt = run[s] + both[s][k]
                if len(shards_q[s]) < half - s:
                    nxt = jnp.concatenate([nxt, shards_q[s][-1]], axis=1)
                run[s] = lax.ppermute(nxt, "fsdp", rings[s])
    place = (jnp.arange(chunk) // rows == core).astype(F32)[:, None]
    errors = jnp.concatenate([error_in[0], error_in[0]], axis=0) * place
    run = [run[s] + jnp.where(rising[s], 0.0, both[s][half - 1]) for s in range(2)]
    run = jnp.concatenate(run, axis=1) + errors
    got = lax.ppermute(run, "fsdp", swap)

    width = mid // own_q * SLOT
    sent, merged = pl.pallas_call(
        functools.partial(pack_kernel, islands, piece),
        out_shape=(jax.ShapeDtypeStruct((islands, 8, width), F32), jax.ShapeDtypeStruct((8, mid), F32)),
        in_specs=[SMEM, SMEM] + [VMEM] * (3 + chips - 1),
        out_specs=(VMEM, VMEM),
        scratch_shapes=[pltpu.VMEM((8, f_blk), F32)],
        compiler_params=PARAMS,
        name="pack",
    )(jnp.stack([y, core]), mine[None], run, got, q_t, *shards_q[0], *shards_q[1])
    mean = jnp.sum(lax.all_to_all(sent, "dp", 0, 0, tiled=True), axis=0)
    mean = lax.all_to_all(jnp.broadcast_to(mean[None], (groups, 8, width)), "fsdp", 0, 0, tiled=True)
    sent = pl.pallas_call(
        functools.partial(factor_kernel, piece),
        out_shape=jax.ShapeDtypeStruct((islands, 8, width + LANES), F32),
        in_specs=[SMEM, VMEM],
        out_specs=VMEM,
        compiler_params=PARAMS,
        name="factor",
    )(f[None], mean)
    got = lax.all_to_all(sent, "dp", 0, 0, tiled=True)
    error_out, approx, q_next = pl.pallas_call(
        functools.partial(unpack_kernel, piece),
        out_shape=(
            jax.ShapeDtypeStruct((rows, f_blk), F32),
            jax.ShapeDtypeStruct((rows, cols), F32),
            jax.ShapeDtypeStruct((rank, own_q), F32),
        ),
        in_specs=[SMEM, VMEM, VMEM],
        out_specs=(VMEM, VMEM, VMEM),
        scratch_shapes=[pltpu.VMEM((8, mid), F32)],
        compiler_params=PARAMS,
        name="unpack",
    )(i[None], got, merged)
    return (error_out[None], approx, q_next.T)


def solution(mesh):
    return jax.shard_map(
        shards,
        mesh=mesh,
        in_specs=(
            P("dp", "fsdp", None),
            P("dp", "fsdp", None),
            P("dp", "fsdp", None),
            P("fsdp", None),
            P(),
            P(),
        ),
        out_specs=(P("dp", "fsdp", None), P("fsdp", "dp"), P("fsdp", None)),
        check_vma=False,
    )
```

time: 609 us -> 138 us (0.23)
  waiting for transfers between devices: 447 us -> 24.5 us
  blocking collectives: 118 us -> 57.1 us
  starting transfers between devices: 0.12 us -> 39.1 us
  between operations: 14.5 us -> 2.29 us
  other arithmetic: 11.4 us -> 1.39 us
  matrix products: 14.3 us -> 4.84 us
  Pallas kernels: 0 us -> 7.24 us
    psum x1 -> x0, waiting for transfers between devices: 275 us -> none  [shards(): q_whole = lax.psum(local_q, ('fsdp', 'dp')) / total]
    unnamed x4 -> x0, waiting for transfers between devices: 128 us -> none
    psum x2 -> x0, blocking collectives: 118 us -> none  [the longest x1 61.9 us: shards(): p_sum = lax.psum(local_p, 'dp') / total]
    all_to_all x0 -> x3, blocking collectives: none -> 57.1 us  [the longest x1 25.5 us: shards(): mean = jnp.sum(lax.all_to_all(sent, 'dp', 0, 0, tiled=True), axis=0)]
    all_gather x1 -> x0, waiting for transfers between devices: 44.3 us -> none  [shards(): whole_q = lax.all_gather(q_warm, 'fsdp', axis=0, tiled=True)]
    ppermute x0 -> x11, starting transfers between devices: none -> 39.1 us  [the longest x6 16.8 us: shards(): run[s] = lax.ppermute(nxt, 'fsdp', rings[s])]
    ppermute x0 -> x11, waiting for transfers between devices: none -> 24.5 us  [the longest x6 18.5 us: shards(): run[s] = lax.ppermute(nxt, 'fsdp', rings[s])]
    dot_general x5, matrix products: 13.5 us -> 4.84 us  [the longest x4 4.65 us: product(): return jnp.einsum('td,tf->df', x, z, preferred_element_type=F32)]
  transfers between devices with their start and end apart: 3 -> 11, of which waited for: 3 -> 7; matrix products, arithmetic and copies ran while one was open for 0% -> 2% of each run, Pallas kernels for 0% -> 0%
where the time goes in v2:
time: 138 us; the launch traced here: 137 us
  blocking collectives  57.1 us (41%)
  starting transfers between devices  39.1 us (28%)
  waiting for transfers between devices  24.5 us (18%)
  Pallas kernels  7.24 us (5%)
  matrix products  4.84 us (4%)
  between operations  2.29 us (2%)
  other arithmetic  1.39 us (1%)
    all_to_all x1, blocking collectives, shards(): mean = jnp.sum(lax.all_to_all(sent, 'dp', 0, 0, tiled=True), axis=0)  25.5 us
    ppermute x6, waiting for transfers between devices, shards(): run[s] = lax.ppermute(nxt, 'fsdp', rings[s])  18.5 us
    all_to_all x1, blocking collectives, shards(): got = lax.all_to_all(sent, 'dp', 0, 0, tiled=True)  18 us
    ppermute x6, starting transfers between devices, shards(): run[s] = lax.ppermute(nxt, 'fsdp', rings[s])  16.8 us
    all_to_all x1, blocking collectives, shards(): lax.all_to_all(jnp.broadcast_to(mean[None], (groups, 8, width)), 'fsdp',...  13.6 us
    ppermute x2, starting transfers between devices, shards(): got = lax.ppermute(product(other, z), 'fsdp', swap)  10.8 us
    ppermute x2, starting transfers between devices, shards(): lax.ppermute(jnp.concatenate([both[s][half - 1], held], axis=1), 'fsdp',...  6.49 us
    ppermute x1, starting transfers between devices, shards(): got = lax.ppermute(run, 'fsdp', swap)  5.04 us
  transfers between devices with their start and end apart: 11, of which 7 were waited for; matrix products, arithmetic and copies ran while one was open for 2% of the time, Pallas kernels for 0%

profile of v2, /device:TPU:1, one launch (start us, length us, event | category | flops | bytes accessed | tf_op | source)
XLA Modules:
  0.0 137.3 jit_solution(17545507645055511540)
XLA Ops:
  1.6 2.0 %fusion.3 = f32[32,7168]{1,0:T(8,128)S(1)} fusion(bf16[128,14336]{1,0:T(8,128)(2,1)} %bitcast.30, bf16[128,64]{0,1:T(8,128)(2,1)S(1)} %fusion.6), kind=kOutput, calls=%fused_computation.5 | convolution fusion | flops 58720256 | bytes 2760704 | tf_op jit(solution)/shard_map/td,tf->df/dot_general | solution.py:193
  3.6 8.8 %collective-permute-start = (f32[32,7168]{1,0:T(8,128)S(1)}, f32[32,7168]{1,0:T(8,128)S(1)}, u32[]{:S(2)}, u32[]{:S(2)}) collective-permute-start(f32[32,7168]{1,0:T(8,128)S(1)} %fusion.3), channel_id=1, source_target_pairs={{0,32},{32,0},{64,96},{96,64},{128,160},{160,128},{192,224},{224,1... | collective-permute-start | bytes 2752520 | tf_op jit(solution)/shard_map/ppermute | solution.py:205
  12.4 1.9 %fusion = f32[32,7168]{1,0:T(8,128)S(1)} fusion(bf16[128,14336]{1,0:T(8,128)(2,1)} %bitcast.31, bf16[128,64]{0,1:T(8,128)(2,1)S(1)} %fusion.6), kind=kOutput, calls=%fused_computation.2 | convolution fusion | flops 58720256 | bytes 2760704 | tf_op jit(solution)/shard_map/td,tf->df/dot_general | solution.py:193
  14.3 2.1 %collective-permute-start.5 = (f32[32,7168]{1,0:T(8,128)S(1)}, f32[32,7168]{1,0:T(8,128)S(1)}, u32[]{:S(2)}, u32[]{:S(2)}) collective-permute-start(f32[32,7168]{1,0:T(8,128)S(1)} %fusion), channel_id=1, source_target_pairs={{0,32},{32,0},{64,96},{96,64},{128,160},{160,128},{192,224},{224,1... | collective-permute-start | bytes 2752520 | tf_op jit(solution)/shard_map/ppermute | solution.py:205
  16.7 2.0 %collective-permute-done.5 = f32[32,7168]{1,0:T(8,128)S(1)} collective-permute-done((f32[32,7168]{1,0:T(8,128)S(1)}, f32[32,7168]{1,0:T(8,128)S(1)}, u32[]{:S(2)}, u32[]{:S(2)}) %collective-permute-start.5) | collective-permute-done | bytes 917536 | tf_op jit(solution)/shard_map/ppermute | solution.py:205
  19.2 1.9 %collective-permute-start.6 = (f32[8,10752]{1,0:T(8,128)S(1)}, f32[8,10752]{1,0:T(8,128)S(1)}, u32[]{:S(2)}, u32[]{:S(2)}) collective-permute-start(f32[8,10752]{1,0:T(8,128)S(1)} %get-tuple-element.16), channel_id=1, source_target_pairs={{0,448},{64,0},{128,64},{192,128},{256,192},{320,256},{384,320},{4... | collective-permute-start | bytes 1032200 | tf_op jit(solution)/shard_map/ppermute | solution.py:207
  21.2 4.6 %collective-permute-start.1 = (f32[8,10752]{1,0:T(8,128)S(1)}, f32[8,10752]{1,0:T(8,128)S(1)}, u32[]{:S(2)}, u32[]{:S(2)}) collective-permute-start(f32[8,10752]{1,0:T(8,128)S(1)} %get-tuple-element.15), channel_id=1, source_target_pairs={{0,64},{64,128},{128,192},{192,256},{256,320},{320,384},{384,448},... | collective-permute-start | bytes 1032200 | tf_op jit(solution)/shard_map/ppermute | solution.py:207
  25.8 4.0 %collective-permute-done.6 = f32[8,10752]{1,0:T(8,128)S(1)} collective-permute-done((f32[8,10752]{1,0:T(8,128)S(1)}, f32[8,10752]{1,0:T(8,128)S(1)}, u32[]{:S(2)}, u32[]{:S(2)}) %collective-permute-start.6) | collective-permute-done | bytes 344096 | tf_op jit(solution)/shard_map/ppermute | solution.py:207
  29.9 1.9 %collective-permute-start.7 = (f32[8,10752]{1,0:T(8,128)S(1)}, f32[8,10752]{1,0:T(8,128)S(1)}, u32[]{:S(2)}, u32[]{:S(2)}) collective-permute-start(f32[8,10752]{1,0:T(8,128)S(1)} %pad_maximum_fusion.5), channel_id=1, source_target_pairs={{0,448},{64,0},{128,64},{192,128},{256,192},{320,256},{384,320},{4... | collective-permute-start | bytes 1032200 | tf_op jit(solution)/shard_map/ppermute | solution.py:220
  31.9 4.7 %collective-permute-start.2 = (f32[8,10752]{1,0:T(8,128)S(1)}, f32[8,10752]{1,0:T(8,128)S(1)}, u32[]{:S(2)}, u32[]{:S(2)}) collective-permute-start(f32[8,10752]{1,0:T(8,128)S(1)} %pad_maximum_fusion.2), channel_id=1, source_target_pairs={{0,64},{64,128},{128,192},{192,256},{256,320},{320,384},{384,448},... | collective-permute-start | bytes 1032200 | tf_op jit(solution)/shard_map/ppermute | solution.py:220
  36.6 2.8 %collective-permute-done.7 = f32[8,10752]{1,0:T(8,128)S(1)} collective-permute-done((f32[8,10752]{1,0:T(8,128)S(1)}, f32[8,10752]{1,0:T(8,128)S(1)}, u32[]{:S(2)}, u32[]{:S(2)}) %collective-permute-start.7) | collective-permute-done | bytes 344096 | tf_op jit(solution)/shard_map/ppermute | solution.py:220
  39.5 1.9 %collective-permute-start.8 = (f32[8,10752]{1,0:T(8,128)S(1)}, f32[8,10752]{1,0:T(8,128)S(1)}, u32[]{:S(2)}, u32[]{:S(2)}) collective-permute-start(f32[8,10752]{1,0:T(8,128)S(1)} %pad_maximum_fusion.6), channel_id=1, source_target_pairs={{0,448},{64,0},{128,64},{192,128},{256,192},{320,256},{384,320},{4... | collective-permute-start | bytes 1032200 | tf_op jit(solution)/shard_map/ppermute | solution.py:220
  43.2 2.9 %collective-permute-start.3 = (f32[8,10752]{1,0:T(8,128)S(1)}, f32[8,10752]{1,0:T(8,128)S(1)}, u32[]{:S(2)}, u32[]{:S(2)}) collective-permute-start(f32[8,10752]{1,0:T(8,128)S(1)} %pad_maximum_fusion.3), channel_id=1, source_target_pairs={{0,64},{64,128},{128,192},{192,256},{256,320},{320,384},{384,448},... | collective-permute-start | bytes 1032200 | tf_op jit(solution)/shard_map/ppermute | solution.py:220
  46.1 2.6 %collective-permute-done.8 = f32[8,10752]{1,0:T(8,128)S(1)} collective-permute-done((f32[8,10752]{1,0:T(8,128)S(1)}, f32[8,10752]{1,0:T(8,128)S(1)}, u32[]{:S(2)}, u32[]{:S(2)}) %collective-permute-start.8) | collective-permute-done | bytes 344096 | tf_op jit(solution)/shard_map/ppermute | solution.py:220
  48.7 1.9 %collective-permute-start.9 = (f32[8,7168]{1,0:T(8,128)S(1)}, f32[8,7168]{1,0:T(8,128)S(1)}, u32[]{:S(2)}, u32[]{:S(2)}) collective-permute-start(f32[8,7168]{1,0:T(8,128)S(1)} %slice_add_fusion), channel_id=1, source_target_pairs={{0,448},{64,0},{128,64},{192,128},{256,192},{320,256},{384,320},{4... | collective-permute-start | bytes 688136 | tf_op jit(solution)/shard_map/ppermute | solution.py:220
  50.7 4.1 %collective-permute-done.3 = f32[8,10752]{1,0:T(8,128)S(1)} collective-permute-done((f32[8,10752]{1,0:T(8,128)S(1)}, f32[8,10752]{1,0:T(8,128)S(1)}, u32[]{:S(2)}, u32[]{:S(2)}) %collective-permute-start.3) | collective-permute-done | bytes 344096 | tf_op jit(solution)/shard_map/ppermute | solution.py:220
  54.9 3.3 %collective-permute-start.4 = (f32[8,10752]{1,0:T(8,128)S(1)}, f32[8,10752]{1,0:T(8,128)S(1)}, u32[]{:S(2)}, u32[]{:S(2)}) collective-permute-start(f32[8,10752]{1,0:T(8,128)S(1)} %pad_maximum_fusion.4), channel_id=1, source_target_pairs={{0,64},{64,128},{128,192},{192,256},{256,320},{320,384},{384,448},... | collective-permute-start | bytes 1032200 | tf_op jit(solution)/shard_map/ppermute | solution.py:220
  58.3 7.3 %collective-permute-done.4 = f32[8,10752]{1,0:T(8,128)S(1)} collective-permute-done((f32[8,10752]{1,0:T(8,128)S(1)}, f32[8,10752]{1,0:T(8,128)S(1)}, u32[]{:S(2)}, u32[]{:S(2)}) %collective-permute-start.4) | collective-permute-done | bytes 344096 | tf_op jit(solution)/shard_map/ppermute | solution.py:220
  65.8 5.0 %collective-permute-start.10 = (f32[8,14336]{1,0:T(8,128)S(1)}, f32[8,14336]{1,0:T(8,128)S(1)}, u32[]{:S(2)}, u32[]{:S(2)}) collective-permute-start(f32[8,14336]{1,0:T(8,128)S(1)} %maximum_add_fusion.own_ref), channel_id=1, source_target_pairs={{0,32},{32,0},{64,96},{96,64},{128,160},{160,128},{192,224},{224,1... | collective-permute-start | bytes 1376264 | tf_op jit(solution)/shard_map/ppermute | solution.py:225
  72.8 1.7 %pack.1 = (f32[32,8,256]{2,1,0:T(8,128)S(1)}, f32[8,7168]{1,0:T(8,128)S(1)}) custom-call(s32[2]{0:T(128)S(1)} %pad_add_fusion.where_ref, f32[1]{0:T(128)} %bitcast.4.mine_ref, f32[8,14336]{1,0:T(8,128)S(1)} %maximum_add_fusion.own_ref, f32[8,14336]{1,0:T(8,128)S(1)} %collective-permute-done.10.got_ref, f32[32,896]{1,0:T(8,128)S(1)} %bitcast.29, ...), custom_call_target="tpu_custom_call" | custom-call | tf_op jit(solution)/shard_map/pack/pallas_call | solution.py:228
  74.6 25.5 %all_to_all.15 = f32[32,8,256]{2,1,0:T(8,128)S(1)} all-to-all(f32[32,8,256]{2,1,0:T(8,128)S(1)} %get-tuple-element.8), channel_id=1, replica_groups=mesh['fsdp'=16,'dp'=32] {'dp'}, dimensions={0} | all-to-all | bytes 524288 | tf_op jit(solution)/shard_map/all_to_all | solution.py:237
  100.2 13.6 %all_to_all.16.mean_ref = f32[16,8,256]{2,1,0:T(8,128)S(1)} all-to-all(f32[16,8,256]{2,1,0:T(8,128)S(1)} %broadcast_in_dim.39), channel_id=1, replica_groups=mesh['fsdp'=16,'dp'=32] {'fsdp'}, dimensions={0} | all-to-all | bytes 262144 | tf_op jit(solution)/shard_map/all_to_all | solution.py:238
  113.8 4.3 %factor.1 = f32[32,8,384]{2,1,0:T(8,128)S(1)} custom-call(s32[1]{0:T(128)} %bitcast.1.where_ref, f32[16,8,256]{2,1,0:T(8,128)S(1)} %all_to_all.16.mean_ref), custom_call_target="tpu_custom_call" | custom-call | tf_op jit(solution)/shard_map/factor/pallas_call | solution.py:239
  118.1 18.0 %all_to_all.17.got_ref = f32[32,8,384]{2,1,0:T(8,128)S(1)} all-to-all(f32[32,8,384]{2,1,0:T(8,128)S(1)} %factor.1), channel_id=1, replica_groups=mesh['fsdp'=16,'dp'=32] {'dp'}, dimensions={0} | all-to-all | bytes 786432 | tf_op jit(solution)/shard_map/all_to_all | solution.py:247
  (55 shorter events, 5.9 us)
Async XLA Ops:
  0.6 0.7 copy-start
  1.4 15.0 %copy-start.2 = (bf16[1,128,14336]{2,1,0:T(8,128)(2,1)S(1)}, bf16[1,128,14336]{2,1,0:T(8,128)(2,1)}, u32[]{:S(2)}) copy-start(bf16[1,128,14336]{2,1,0:T(8,128)(2,1)} %param.7) | copy-start | bytes 11010052
  3.6 12.7 %collective-permute-start = (f32[32,7168]{1,0:T(8,128)S(1)}, f32[32,7168]{1,0:T(8,128)S(1)}, u32[]{:S(2)}, u32[]{:S(2)}) collective-permute-start(f32[32,7168]{1,0:T(8,128)S(1)} %fusion.3), channel_id=1, source_target_pairs={{0,32},{32,0},{64,96},{96,64},{128,160},{160,128},{192,224},{224,1... | collective-permute-start | bytes 2752520 | tf_op jit(solution)/shard_map/ppermute | solution.py:205
  14.2 4.9 %copy-start.1 = (f32[896,32]{0,1:T(8,128)S(1)}, f32[896,32]{0,1:T(8,128)}, u32[]{:S(2)}) copy-start(f32[896,32]{0,1:T(8,128)} %param.9) | copy-start | bytes 344068
  14.3 4.5 %collective-permute-start.5 = (f32[32,7168]{1,0:T(8,128)S(1)}, f32[32,7168]{1,0:T(8,128)S(1)}, u32[]{:S(2)}, u32[]{:S(2)}) collective-permute-start(f32[32,7168]{1,0:T(8,128)S(1)} %fusion), channel_id=1, source_target_pairs={{0,32},{32,0},{64,96},{96,64},{128,160},{160,128},{192,224},{224,1... | collective-permute-start | bytes 2752520 | tf_op jit(solution)/shard_map/ppermute | solution.py:205
  19.2 10.6 %collective-permute-start.6 = (f32[8,10752]{1,0:T(8,128)S(1)}, f32[8,10752]{1,0:T(8,128)S(1)}, u32[]{:S(2)}, u32[]{:S(2)}) collective-permute-start(f32[8,10752]{1,0:T(8,128)S(1)} %get-tuple-element.16), channel_id=1, source_target_pairs={{0,448},{64,0},{128,64},{192,128},{256,192},{320,256},{384,320},{4... | collective-permute-start | bytes 1032200 | tf_op jit(solution)/shard_map/ppermute | solution.py:207
  21.2 10.6 %collective-permute-start.1 = (f32[8,10752]{1,0:T(8,128)S(1)}, f32[8,10752]{1,0:T(8,128)S(1)}, u32[]{:S(2)}, u32[]{:S(2)}) collective-permute-start(f32[8,10752]{1,0:T(8,128)S(1)} %get-tuple-element.15), channel_id=1, source_target_pairs={{0,64},{64,128},{128,192},{192,256},{256,320},{320,384},{384,448},... | collective-permute-start | bytes 1032200 | tf_op jit(solution)/shard_map/ppermute | solution.py:207
  29.9 9.5 %collective-permute-start.7 = (f32[8,10752]{1,0:T(8,128)S(1)}, f32[8,10752]{1,0:T(8,128)S(1)}, u32[]{:S(2)}, u32[]{:S(2)}) collective-permute-start(f32[8,10752]{1,0:T(8,128)S(1)} %pad_maximum_fusion.5), channel_id=1, source_target_pairs={{0,448},{64,0},{128,64},{192,128},{256,192},{320,256},{384,320},{4... | collective-permute-start | bytes 1032200 | tf_op jit(solution)/shard_map/ppermute | solution.py:220
  31.9 33.8 %copy-start.3 = (f32[1,4,14336]{2,1,0:T(4,128)S(1)}, f32[1,4,14336]{2,1,0:T(4,128)}, u32[]{:S(2)}) copy-start(f32[1,4,14336]{2,1,0:T(4,128)} %param.8) | copy-start | bytes 688132
  31.9 11.2 %collective-permute-start.2 = (f32[8,10752]{1,0:T(8,128)S(1)}, f32[8,10752]{1,0:T(8,128)S(1)}, u32[]{:S(2)}, u32[]{:S(2)}) collective-permute-start(f32[8,10752]{1,0:T(8,128)S(1)} %pad_maximum_fusion.2), channel_id=1, source_target_pairs={{0,64},{64,128},{128,192},{192,256},{256,320},{320,384},{384,448},... | collective-permute-start | bytes 1032200 | tf_op jit(solution)/shard_map/ppermute | solution.py:220
  39.4 31.4 %copy-start.4 = (s32[32]{0:T(128)S(1)}, s32[32]{0:T(128)}, u32[]{:S(2)}) copy-start(s32[32]{0:T(128)} %param.10) | copy-start | bytes 388
  39.4 31.4 %copy-start.5 = (s32[32]{0:T(128)S(1)}, s32[32]{0:T(128)}, u32[]{:S(2)}) copy-start(s32[32]{0:T(128)} %param.11) | copy-start | bytes 388
  39.5 9.2 %collective-permute-start.8 = (f32[8,10752]{1,0:T(8,128)S(1)}, f32[8,10752]{1,0:T(8,128)S(1)}, u32[]{:S(2)}, u32[]{:S(2)}) collective-permute-start(f32[8,10752]{1,0:T(8,128)S(1)} %pad_maximum_fusion.6), channel_id=1, source_target_pairs={{0,448},{64,0},{128,64},{192,128},{256,192},{320,256},{384,320},{4... | collective-permute-start | bytes 1032200 | tf_op jit(solution)/shard_map/ppermute | solution.py:220
  43.2 11.6 %collective-permute-start.3 = (f32[8,10752]{1,0:T(8,128)S(1)}, f32[8,10752]{1,0:T(8,128)S(1)}, u32[]{:S(2)}, u32[]{:S(2)}) collective-permute-start(f32[8,10752]{1,0:T(8,128)S(1)} %pad_maximum_fusion.3), channel_id=1, source_target_pairs={{0,64},{64,128},{128,192},{192,256},{256,320},{320,384},{384,448},... | collective-permute-start | bytes 1032200 | tf_op jit(solution)/shard_map/ppermute | solution.py:220
  48.7 9.5 %collective-permute-start.9 = (f32[8,7168]{1,0:T(8,128)S(1)}, f32[8,7168]{1,0:T(8,128)S(1)}, u32[]{:S(2)}, u32[]{:S(2)}) collective-permute-start(f32[8,7168]{1,0:T(8,128)S(1)} %slice_add_fusion), channel_id=1, source_target_pairs={{0,448},{64,0},{128,64},{192,128},{256,192},{320,256},{384,320},{4... | collective-permute-start | bytes 688136 | tf_op jit(solution)/shard_map/ppermute | solution.py:220
  54.9 10.7 %collective-permute-start.4 = (f32[8,10752]{1,0:T(8,128)S(1)}, f32[8,10752]{1,0:T(8,128)S(1)}, u32[]{:S(2)}, u32[]{:S(2)}) collective-permute-start(f32[8,10752]{1,0:T(8,128)S(1)} %pad_maximum_fusion.4), channel_id=1, source_target_pairs={{0,64},{64,128},{128,192},{192,256},{256,320},{320,384},{384,448},... | collective-permute-start | bytes 1032200 | tf_op jit(solution)/shard_map/ppermute | solution.py:220
  65.8 7.1 %collective-permute-start.10 = (f32[8,14336]{1,0:T(8,128)S(1)}, f32[8,14336]{1,0:T(8,128)S(1)}, u32[]{:S(2)}, u32[]{:S(2)}) collective-permute-start(f32[8,14336]{1,0:T(8,128)S(1)} %maximum_add_fusion.own_ref), channel_id=1, source_target_pairs={{0,32},{32,0},{64,96},{96,64},{128,160},{160,128},{192,224},{224,1... | collective-permute-start | bytes 1376264 | tf_op jit(solution)/shard_map/ppermute | solution.py:225

commit v3 on v2

v3 whole, which is shorter than its diff:
```python
import functools

import jax
import jax.numpy as jnp
from jax import lax
from jax.experimental import pallas as pl
from jax.experimental.pallas import tpu as pltpu
from jax.sharding import PartitionSpec as P

HIGHEST = lax.Precision.HIGHEST
LANES = 128
SLOT = 32
F32 = jnp.float32


def iota(shape, axis):
    return lax.broadcasted_iota(jnp.int32, shape, axis)


def contract(x, z, dims):
    return lax.dot_general(x, z, ((dims[:1], dims[1:]), ((), ())), precision=HIGHEST, preferred_element_type=F32)


def product_kernel(splits, where_ref, a_ref, c_ref, error_ref, *refs):
    *out_refs, held_ref, sems = refs
    side = where_ref[0]
    span = error_ref.shape[1] // (2 * sems.shape[0])
    starts = [pl.multiple_of((2 * j + side) * span, LANES) for j in range(sems.shape[0])]
    copies = []
    for j, at in enumerate(starts):
        copies.append(pltpu.make_async_copy(c_ref.at[:, pl.ds(at, span)], held_ref.at[:, j * span : (j + 1) * span], sems.at[j]))
        copies[j].start()
    chunk = error_ref.shape[0]
    a = a_ref[...]
    for j in range(0, len(copies), 2):
        copies[j].wait()
        copies[j + 1].wait()
        cols = slice(j * span, (j + 2) * span)
        out = jnp.dot(a, held_ref[:, cols], preferred_element_type=F32)
        last = out[-chunk:] + jnp.concatenate([error_ref[:, pl.ds(at, span)] for at in starts[j : j + 2]], axis=1)
        first = 0
        for n, size in enumerate(splits):
            if n < len(splits) - 1:
                out_refs[n][:, cols] = out[first : first + size]
            else:
                if size > chunk:
                    out_refs[n][: size - chunk, cols] = out[first : first + size - chunk]
                out_refs[n][size - chunk :, cols] = last
            first += size


def pack_kernel(n_dp, piece, where_ref, mine_ref, long_ref, short_ref, own_ref, q_ref, *refs):
    *shard_refs, sent_ref, kept_ref, given_ref, sum_ref = refs
    y, core = where_ref[0], where_ref[1]
    chips, span = len(shard_refs) + 1, q_ref.shape[1]
    mid = own_ref.shape[1]
    total = long_ref[:, :mid] + short_ref[:, :mid] + own_ref[...]
    sum_ref[...] = total
    upper, lower = total[:4], total[4:]
    kept_ref[...] = jnp.where(core == 0, upper, lower)
    given_ref[...] = jnp.where(core == 0, lower, upper)

    rank = q_ref.shape[0]
    parts = jnp.zeros((8, rank), F32)
    for k in range(chips):
        if k == 0:
            shard, chip = q_ref[...], y
        else:
            held = shard_refs[k - 1][:, mid:]
            shard = jnp.concatenate([held[:, a * span : (a + 1) * span] for a in range(rank // 8)], axis=0)
            step = k if k <= chips // 2 else chips // 2 - k
            chip = lax.rem(y + chips - jnp.where(core == 0, step, -step), chips)
        start = pl.multiple_of(chip * span, LANES)
        parts = parts + contract(sum_ref[:, pl.ds(start, span)], shard, (1, 1))

    mine = mine_ref[0]
    scaled = total * mine

    slots = mid // span
    width = slots * SLOT
    spot = (iota((rank, width), 1) // SLOT) * (SLOT - piece) + iota((rank, width), 1) % SLOT - piece
    place = ((iota((rank, width), 1) % SLOT >= piece) & (spot == iota((rank, width), 0))).astype(F32)
    base = contract(parts * mine, place, (1, 0))
    lane = iota((8, LANES), 1)
    for k in range(n_dp):
        first = (k * piece) // LANES
        for v in range(width // LANES):
            out = base[:, v * LANES : (v + 1) * LANES]
            for b in range(LANES // SLOT):
                f = v * (LANES // SLOT) + b
                for w in range(first, (k * piece + piece - 1) // LANES + 1):
                    src = f * span + w * LANES
                    at = k * piece - w * LANES
                    moved = pltpu.roll(scaled[:, src : src + LANES], (b * SLOT - at) % LANES, 1)
                    lo = b * SLOT + max(0, -at)
                    hi = b * SLOT + min(piece, LANES - at)
                    out = jnp.where((lane >= lo) & (lane < hi), moved, out)
            sent_ref[k, :, v * LANES : (v + 1) * LANES] = out


def factor_kernel(piece, where_ref, mean_ref, sent_ref):
    f = where_ref[3]
    groups, _, width = mean_ref.shape
    slots = width // SLOT
    rank = slots * (SLOT - piece)
    d_blk = groups * 4
    mean = mean_ref[...].reshape(groups * 8, width)
    lane_i, sub_i = iota((width, LANES), 0), iota((width, LANES), 1)
    pick = ((lane_i % SLOT >= piece) & ((lane_i // SLOT) * (SLOT - piece) + lane_i % SLOT - piece == sub_i)).astype(F32)
    p_all = contract(mean, pick, (1, 0)).reshape(groups // 2, 2, 8, LANES)
    p_sum = (p_all[:, 0] + p_all[:, 1]).reshape(d_blk, LANES)

    sub, lane = iota((d_blk, LANES), 0), iota((d_blk, LANES), 1)
    wide = p_sum + (lane == sub + rank).astype(F32)
    a = contract(p_sum, wide, (0, 0))[:rank]
    row_i = iota((rank, LANES), 0)
    for k in range(rank):
        pivot = a[k : k + 1, k : k + 1]
        inv = lax.rsqrt(pivot)
        inv = inv * (1.5 - 0.5 * pivot * inv * inv)
        row = a[k : k + 1, :] * inv
        col = jnp.where(row_i[:, :1] > k, a[:, k : k + 1] * inv, 0.0)
        a = jnp.where(row_i == k, row, a - col * row)

    approx = jnp.zeros((8, width), F32)
    halves = []
    src, dst = iota((LANES, groups * 8), 0) - rank, iota((LANES, groups * 8), 1)
    for h in range(2):
        spread = ((dst // 8 % 2 == h) & (src == dst // 16 * 8 + dst % 8)).astype(F32)
        q_half = contract(contract(a, spread, (1, 0)), mean, (1, 0))
        own = ((iota((LANES, 8), 1) // 4 == h) & (iota((LANES, 8), 0) - rank == f * 4 + iota((LANES, 8), 1) % 4)).astype(F32)
        approx = approx + contract(contract(a, own, (1, 0)), q_half, (0, 0))
        halves.append(q_half)
    q_mine = jnp.where(lax.rem(f, 2) == 0, halves[0], halves[1])
    q_mine = pltpu.roll(q_mine, lax.rem(width - f // 2 * SLOT, width), 1)[:, :LANES]
    lane = iota((8, LANES), 1)
    q_out = jnp.zeros((8, LANES), F32)
    for b in range(rank // 8):
        q_out = jnp.where(lane // SLOT == b, pltpu.roll(q_mine[b * 8 : b * 8 + 8], b * SLOT, 1), q_out)
    for k in range(sent_ref.shape[0]):
        sent_ref[k, :, :width] = approx
        sent_ref[k, :, width:] = q_out


def unpack_kernel(piece, where_ref, got_ref, kept_ref, got_row_ref, error_ref, approx_ref, q_ref, whole_ref):
    i, core = where_ref[2], where_ref[1]
    n_dp, _, width = got_ref.shape
    width -= LANES
    span = q_ref.shape[1]
    slots = width // SLOT
    lane = iota((8, LANES), 1)
    for f in range(slots):
        v, b = f * SLOT // LANES, f % (LANES // SLOT)
        for w in range(span // LANES):
            out = jnp.zeros((8, LANES), F32)
            for k in range(w * LANES // piece, ((w + 1) * LANES - 1) // piece + 1):
                at = k * piece - w * LANES
                moved = pltpu.roll(got_ref[k, :, v * LANES : (v + 1) * LANES], (at - b * SLOT) % LANES, 1)
                out = jnp.where((lane >= at) & (lane < at + piece), moved, out)
            whole_ref[:, f * span + w * LANES : f * span + (w + 1) * LANES] = out
    for b in range(q_ref.shape[0] // 8):
        for w in range(span // LANES):
            out = jnp.zeros((8, LANES), F32)
            for k in range(w * LANES // piece, ((w + 1) * LANES - 1) // piece + 1):
                at = k * piece - w * LANES
                moved = pltpu.roll(got_ref[k, :, width:], (at - b * SLOT) % LANES, 1)
                out = jnp.where((lane >= at) & (lane < at + piece), moved, out)
            q_ref[b * 8 : b * 8 + 8, w * LANES : (w + 1) * LANES] = out
    for f in range(2 * slots):
        h, at = f % 2, f // 2 * span
        merged = jnp.where(core == h, kept_ref[:, at : at + span], got_row_ref[:, at : at + span])
        error_ref[:, f * span : (f + 1) * span] = merged - whole_ref[4 * h : 4 * h + 4, at : at + span]
    cols = approx_ref.shape[1]
    f, odd = i // 2, lax.rem(i, 2)
    start = pl.multiple_of(f // 2 * span + odd * (cols // LANES * LANES), LANES)
    window = whole_ref[:, pl.ds(start, cols + LANES // 2)]
    window = jnp.where(odd == 0, window, pltpu.roll(window, cols, 1))
    window = jnp.where(lax.rem(f, 2) == 0, window[:4], window[4:])
    approx_ref[...] = window[:, :cols]


VMEM = pl.BlockSpec(memory_space=pltpu.VMEM)
SMEM = pl.BlockSpec(memory_space=pltpu.SMEM)
PARAMS = pltpu.CompilerParams(vmem_limit_bytes=8 * 2**20)


def shards(acts, cot, error_in, q_warm, quorum, counts):
    groups = lax.axis_size("fsdp")
    islands = lax.axis_size("dp")
    chips = groups // 2
    f = lax.axis_index("fsdp")
    i = lax.axis_index("dp")
    y, core = f // 2, f % 2
    a, c = acts[0], cot[0]
    own_q, rank = q_warm.shape
    d_blk, f_blk = a.shape[1], c.shape[1]
    rows = d_blk // groups
    chunk = 2 * rows
    half = chips // 2
    cols = f_blk // islands
    piece = own_q // islands
    mid = f_blk // 2

    weight = (quorum * counts).astype(F32)
    total = jnp.sum(weight)
    mine = jnp.sum(jnp.where(jnp.arange(islands) == i, weight, 0.0)) / total

    swap = [(k, k ^ 1) for k in range(groups)]
    rise = [(2 * k, 2 * ((k + 1) % chips)) for k in range(chips)] + [(2 * k + 1, 2 * ((k - 1) % chips) + 1) for k in range(chips)]
    fall = [(k, j) for j, k in rise]
    where = jnp.stack([y, core, i, f])
    block = jnp.arange(d_blk) // chunk
    ahead = jnp.where(block < half, half - block, block - (chips - 1))

    place = jnp.arange(chunk)[:, None] // rows == core
    errors = jnp.where(place, jnp.concatenate([error_in[0], error_in[0]], axis=0), 0.0)

    def product(side, splits):
        picked = (y + jnp.where(side == 0, ahead, -ahead)) % chips * chunk + jnp.arange(d_blk) % chunk
        onehot = (picked[:, None] == jnp.arange(d_blk)[None, :]).astype(a.dtype)
        chosen = jnp.einsum("nd,td->nt", onehot, a, preferred_element_type=F32).astype(a.dtype)
        return pl.pallas_call(
            functools.partial(product_kernel, splits),
            out_shape=[jax.ShapeDtypeStruct((size, mid), F32) for size in splits],
            in_specs=[SMEM, VMEM, pl.BlockSpec(memory_space=pl.ANY), VMEM],
            out_specs=[VMEM] * len(splits),
            scratch_shapes=[pltpu.VMEM((c.shape[0], mid), c.dtype), pltpu.SemaphoreType.DMA((chips,))],
            compiler_params=pltpu.CompilerParams(vmem_limit_bytes=6 * 2**20),
            name="product",
        )(side[None], chosen, c, errors)

    other_long, other_short = product(1 - core, (half * chunk, half * chunk))
    far, *own = product(core, (chunk,) * chips)
    got_long = lax.ppermute(other_long, "fsdp", swap)
    got_short = lax.ppermute(other_short, "fsdp", swap)
    far = far + got_long[:chunk]
    long = [own[k] + got_long[(k + 1) * chunk : (k + 2) * chunk] for k in range(half - 1)]
    short = [own[half - 1 + k] + got_short[k * chunk : (k + 1) * chunk] for k in range(half)]

    q_t = q_warm.T
    held = q_t.reshape(rank // 8, 8, own_q).transpose(1, 0, 2).reshape(8, rank // 8 * own_q)
    run_long = [lax.ppermute(jnp.concatenate([far, held], axis=1), "fsdp", rise)]
    run_short = []
    for k in range(half - 1):
        last = run_long[-1]
        run_long.append(lax.ppermute(jnp.concatenate([last[:, :mid] + long[k], last[:, mid:]], axis=1), "fsdp", rise))
        if k == 0:
            last = jnp.concatenate([short[0], held], axis=1)
        else:
            last = jnp.concatenate([run_short[-1][:, :mid] + short[k], run_short[-1][:, mid:]], axis=1)
        run_short.append(lax.ppermute(last, "fsdp", fall))

    width = mid // own_q * SLOT
    sent, kept, given = pl.pallas_call(
        functools.partial(pack_kernel, islands, piece),
        out_shape=(
            jax.ShapeDtypeStruct((islands, 8, width), F32),
            jax.ShapeDtypeStruct((rows, mid), F32),
            jax.ShapeDtypeStruct((rows, mid), F32),
        ),
        in_specs=[SMEM, SMEM] + [VMEM] * (4 + chips - 1),
        out_specs=(VMEM, VMEM, VMEM),
        scratch_shapes=[pltpu.VMEM((8, mid), F32)],
        compiler_params=PARAMS,
        name="pack",
    )(where, mine[None], run_long[-1], run_short[-1], short[-1], q_t, *run_long, *run_short)
    got_rows = lax.ppermute(given, "fsdp", swap)
    mean = jnp.sum(lax.all_to_all(sent, "dp", 0, 0, tiled=True), axis=0)
    mean, got_rows = lax.optimization_barrier((mean, got_rows))
    mean = lax.all_to_all(jnp.broadcast_to(mean[None], (groups, 8, width)), "fsdp", 0, 0, tiled=True)
    sent = pl.pallas_call(
        functools.partial(factor_kernel, piece),
        out_shape=jax.ShapeDtypeStruct((islands, 8, width + LANES), F32),
        in_specs=[SMEM, VMEM],
        out_specs=VMEM,
        compiler_params=PARAMS,
        name="factor",
    )(where, mean)
    got = lax.all_to_all(sent, "dp", 0, 0, tiled=True)
    error_out, approx, q_next = pl.pallas_call(
        functools.partial(unpack_kernel, piece),
        out_shape=(
            jax.ShapeDtypeStruct((rows, f_blk), F32),
            jax.ShapeDtypeStruct((rows, cols), F32),
            jax.ShapeDtypeStruct((rank, own_q), F32),
        ),
        in_specs=[SMEM, VMEM, VMEM, VMEM],
        out_specs=(VMEM, VMEM, VMEM),
        scratch_shapes=[pltpu.VMEM((8, mid), F32)],
        compiler_params=PARAMS,
        name="unpack",
    )(where, got, kept, got_rows)
    return (error_out[None], approx, q_next.T)


def solution(mesh):
    return jax.shard_map(
        shards,
        mesh=mesh,
        in_specs=(
            P("dp", "fsdp", None),
            P("dp", "fsdp", None),
            P("dp", "fsdp", None),
            P("fsdp", None),
            P(),
            P(),
        ),
        out_specs=(P("dp", "fsdp", None), P("fsdp", "dp"), P("fsdp", None)),
        check_vma=False,
    )
```

time: 138 us -> 134 us (0.971)
  blocking collectives: 57.1 us -> 46.6 us
  starting transfers between devices: 39.1 us -> 44.8 us
  matrix products: 4.84 us -> 0.39 us
  Pallas kernels: 7.24 us -> 11.6 us
  waiting for transfers between devices: 24.5 us -> 21.6 us
  local copies, waits for them, and re-layouts: 0.74 us -> 2.75 us
  other arithmetic: 1.39 us -> 3.18 us
    all_to_all x1 -> x0, blocking collectives: 25.5 us -> none  [shards(): mean = jnp.sum(lax.all_to_all(sent, 'dp', 0, 0, tiled=True), axis=0)]
    all_to_all x1, blocking collectives: 13.6 us -> 28.5 us  [shards(): lax.all_to_all(jnp.broadcast_to(mean[None], (groups, 8, width)), 'fsdp',...]
    all_to_all x0 -> x1, starting transfers between devices: none -> 5.4 us  [shards(): mean = jnp.sum(lax.all_to_all(sent, 'dp', 0, 0, tiled=True), axis=0)]
    dot_general x5 -> x2, matrix products: 4.84 us -> 0.39 us  [product(): jnp.einsum('nd,td->nt', onehot, a, preferred_element_type=F32)]
    ppermute x11 -> x10, waiting for transfers between devices: 24.5 us -> 20.8 us  [the longest x3 10.4 us: shards(): run_short.append(lax.ppermute(last, 'fsdp', fall))]
    pallas_call x0 -> x2, Pallas kernels: none -> 2.5 us  [product(): pl.pallas_call(functools.partial(product_kernel, splits), out_shape=[jax....]
    unnamed x12, local copies, waits for them, and re-layouts: 0.38 us -> 2.69 us
    ppermute x11 -> x10, starting transfers between devices: 39.1 us -> 39.4 us  [the longest x3 9.85 us: shards(): lax.ppermute(jnp.concatenate([last[:, :mid] + long[k], last[:, mid:]], ax...]
  transfers between devices with their start and end apart: 11 -> 11, of which waited for: 7 -> 9; matrix products, arithmetic and copies ran while one was open for 2% -> 2% of each run, Pallas kernels for 0% -> 1%
where the time goes in v3:
time: 134 us; the launch traced here: 133 us
  blocking collectives  46.6 us (35%)
  starting transfers between devices  44.8 us (33%)
  waiting for transfers between devices  21.6 us (16%)
  Pallas kernels  11.6 us (9%)
  other arithmetic  3.18 us (2%)
  local copies, waits for them, and re-layouts  2.75 us (2%)
  between operations  2.28 us (2%)
    all_to_all x1, blocking collectives, shards(): lax.all_to_all(jnp.broadcast_to(mean[None], (groups, 8, width)), 'fsdp',...  28.5 us
    all_to_all x1, blocking collectives, shards(): got = lax.all_to_all(sent, 'dp', 0, 0, tiled=True)  18.1 us
    ppermute x3, waiting for transfers between devices, shards(): run_short.append(lax.ppermute(last, 'fsdp', fall))  10.4 us
    ppermute x3, starting transfers between devices, shards(): lax.ppermute(jnp.concatenate([last[:, :mid] + long[k], last[:, mid:]], ax...  9.85 us
    ppermute x1, starting transfers between devices, shards(): got_rows = lax.ppermute(given, 'fsdp', swap)  9.59 us
    ppermute x1, starting transfers between devices, shards(): got_long = lax.ppermute(other_long, 'fsdp', swap)  8.91 us
    ppermute x3, starting transfers between devices, shards(): run_short.append(lax.ppermute(last, 'fsdp', fall))  7.2 us
    all_to_all x1, starting transfers between devices, shards(): mean = jnp.sum(lax.all_to_all(sent, 'dp', 0, 0, tiled=True), axis=0)  5.4 us
  transfers between devices with their start and end apart: 11, of which 9 were waited for; matrix products, arithmetic and copies ran while one was open for 2% of the time, Pallas kernels for 1%

profile of v3, /device:TPU:1, one launch (start us, length us, event | category | flops | bytes accessed | tf_op | source)
XLA Modules:
  0.0 133.2 jit_solution(12971036277033676543)
XLA Ops:
  2.7 2.0 %copy-done.1 = bf16[1,128,14336]{2,1,0:T(8,128)(2,1)S(1)} copy-done((bf16[1,128,14336]{2,1,0:T(8,128)(2,1)S(1)}, bf16[1,128,14336]{2,1,0:T(8,128)(2,1)}, u32[]{:S(2)}) %copy-start.1) | copy-done | bytes 3670040
  6.0 8.9 %collective-permute-start = (f32[32,7168]{1,0:T(8,128)S(1)}, f32[32,7168]{1,0:T(8,128)S(1)}, u32[]{:S(2)}, u32[]{:S(2)}) collective-permute-start(f32[32,7168]{1,0:T(8,128)S(1)} %get-tuple-element.22), channel_id=1, source_target_pairs={{0,32},{32,0},{64,96},{96,64},{128,160},{160,128},{192,224},{224,1... | collective-permute-start | bytes 2752520 | tf_op jit(solution)/shard_map/ppermute | solution.py:234
  15.0 1.9 %collective-permute-start.5 = (f32[32,7168]{1,0:T(8,128)S(1)}, f32[32,7168]{1,0:T(8,128)S(1)}, u32[]{:S(2)}, u32[]{:S(2)}) collective-permute-start(f32[32,7168]{1,0:T(8,128)S(1)} %get-tuple-element.27), channel_id=1, source_target_pairs={{0,32},{32,0},{64,96},{96,64},{128,160},{160,128},{192,224},{224,1... | collective-permute-start | bytes 2752520 | tf_op jit(solution)/shard_map/ppermute | solution.py:235
  17.1 1.3 product.2
  19.4 1.9 %collective-permute-start.1 = (f32[8,10752]{1,0:T(8,128)S(1)}, f32[8,10752]{1,0:T(8,128)S(1)}, u32[]{:S(2)}, u32[]{:S(2)}) collective-permute-start(f32[8,10752]{1,0:T(8,128)S(1)} %get-tuple-element.44), channel_id=1, source_target_pairs={{0,64},{64,128},{128,192},{192,256},{256,320},{320,384},{384,448},... | collective-permute-start | bytes 1032200 | tf_op jit(solution)/shard_map/ppermute | solution.py:242
  21.3 3.4 %collective-permute-start.6 = (f32[8,10752]{1,0:T(8,128)S(1)}, f32[8,10752]{1,0:T(8,128)S(1)}, u32[]{:S(2)}, u32[]{:S(2)}) collective-permute-start(f32[8,10752]{1,0:T(8,128)S(1)} %get-tuple-element.43), channel_id=1, source_target_pairs={{64,0},{128,64},{192,128},{256,192},{320,256},{384,320},{448,384},... | collective-permute-start | bytes 1032200 | tf_op jit(solution)/shard_map/ppermute | solution.py:251
  24.7 4.1 %collective-permute-done.1.refs_0_ = f32[8,10752]{1,0:T(8,128)S(1)} collective-permute-done((f32[8,10752]{1,0:T(8,128)S(1)}, f32[8,10752]{1,0:T(8,128)S(1)}, u32[]{:S(2)}, u32[]{:S(2)}) %collective-permute-start.1) | collective-permute-done | bytes 344096 | tf_op jit(solution)/shard_map/ppermute | solution.py:242
  28.9 1.9 %collective-permute-start.2 = (f32[8,10752]{1,0:T(8,128)S(1)}, f32[8,10752]{1,0:T(8,128)S(1)}, u32[]{:S(2)}, u32[]{:S(2)}) collective-permute-start(f32[8,10752]{1,0:T(8,128)S(1)} %pad_maximum_fusion.2), channel_id=1, source_target_pairs={{0,64},{64,128},{128,192},{192,256},{256,320},{320,384},{384,448},... | collective-permute-start | bytes 1032200 | tf_op jit(solution)/shard_map/ppermute | solution.py:246
  30.8 2.1 %collective-permute-done.6.refs_4_ = f32[8,10752]{1,0:T(8,128)S(1)} collective-permute-done((f32[8,10752]{1,0:T(8,128)S(1)}, f32[8,10752]{1,0:T(8,128)S(1)}, u32[]{:S(2)}, u32[]{:S(2)}) %collective-permute-start.6) | collective-permute-done | bytes 344096 | tf_op jit(solution)/shard_map/ppermute | solution.py:251
  33.0 1.9 %collective-permute-start.7 = (f32[8,10752]{1,0:T(8,128)S(1)}, f32[8,10752]{1,0:T(8,128)S(1)}, u32[]{:S(2)}, u32[]{:S(2)}) collective-permute-start(f32[8,10752]{1,0:T(8,128)S(1)} %pad_maximum_fusion.5), channel_id=1, source_target_pairs={{64,0},{128,64},{192,128},{256,192},{320,256},{384,320},{448,384},... | collective-permute-start | bytes 1032200 | tf_op jit(solution)/shard_map/ppermute | solution.py:251
  34.9 1.9 %collective-permute-done.2.refs_1_ = f32[8,10752]{1,0:T(8,128)S(1)} collective-permute-done((f32[8,10752]{1,0:T(8,128)S(1)}, f32[8,10752]{1,0:T(8,128)S(1)}, u32[]{:S(2)}, u32[]{:S(2)}) %collective-permute-start.2) | collective-permute-done | bytes 344096 | tf_op jit(solution)/shard_map/ppermute | solution.py:246
  37.0 3.1 %collective-permute-start.3 = (f32[8,10752]{1,0:T(8,128)S(1)}, f32[8,10752]{1,0:T(8,128)S(1)}, u32[]{:S(2)}, u32[]{:S(2)}) collective-permute-start(f32[8,10752]{1,0:T(8,128)S(1)} %pad_maximum_fusion.3), channel_id=1, source_target_pairs={{0,64},{64,128},{128,192},{192,256},{256,320},{320,384},{384,448},... | collective-permute-start | bytes 1032200 | tf_op jit(solution)/shard_map/ppermute | solution.py:246
  40.1 5.6 %collective-permute-done.7.refs_5_ = f32[8,10752]{1,0:T(8,128)S(1)} collective-permute-done((f32[8,10752]{1,0:T(8,128)S(1)}, f32[8,10752]{1,0:T(8,128)S(1)}, u32[]{:S(2)}, u32[]{:S(2)}) %collective-permute-start.7) | collective-permute-done | bytes 344096 | tf_op jit(solution)/shard_map/ppermute | solution.py:251
  45.8 1.9 %collective-permute-start.8 = (f32[8,10752]{1,0:T(8,128)S(1)}, f32[8,10752]{1,0:T(8,128)S(1)}, u32[]{:S(2)}, u32[]{:S(2)}) collective-permute-start(f32[8,10752]{1,0:T(8,128)S(1)} %pad_maximum_fusion.6), channel_id=1, source_target_pairs={{64,0},{128,64},{192,128},{256,192},{320,256},{384,320},{448,384},... | collective-permute-start | bytes 1032200 | tf_op jit(solution)/shard_map/ppermute | solution.py:251
  48.6 4.8 %collective-permute-start.4 = (f32[8,10752]{1,0:T(8,128)}, f32[8,10752]{1,0:T(8,128)S(1)}, u32[]{:S(2)}, u32[]{:S(2)}) collective-permute-start(f32[8,10752]{1,0:T(8,128)} %pad_maximum_fusion.4), channel_id=1, source_target_pairs={{0,64},{64,128},{128,192},{192,256},{256,320},{320,384},{384,448},... | collective-permute-start | bytes 1032200 | tf_op jit(solution)/shard_map/ppermute | solution.py:246
  55.4 2.8 %collective-permute-done.8.short_ref.refs_6_ = f32[8,10752]{1,0:T(8,128)S(1)} collective-permute-done((f32[8,10752]{1,0:T(8,128)S(1)}, f32[8,10752]{1,0:T(8,128)S(1)}, u32[]{:S(2)}, u32[]{:S(2)}) %collective-permute-start.8) | collective-permute-done | bytes 344096 | tf_op jit(solution)/shard_map/ppermute | solution.py:251
  58.2 3.4 %collective-permute-done.4.long_ref.refs_3_ = f32[8,10752]{1,0:T(8,128)S(1)} collective-permute-done((f32[8,10752]{1,0:T(8,128)}, f32[8,10752]{1,0:T(8,128)S(1)}, u32[]{:S(2)}, u32[]{:S(2)}) %collective-permute-start.4) | collective-permute-done | bytes 344096 | tf_op jit(solution)/shard_map/ppermute | solution.py:246
  61.6 2.4 %pack.1 = (f32[32,8,256]{2,1,0:T(8,128)}, f32[4,7168]{1,0:T(4,128)S(1)}, f32[4,7168]{1,0:T(4,128)S(1)}) custom-call(s32[4]{0:T(128)S(1)} %pad_add_fusion.where_ref, f32[1]{0:T(128)} %bitcast.4.mine_ref, f32[8,10752]{1,0:T(8,128)S(1)} %collective-permute-done.4.long_ref.refs_3_, f32[8,10752]{1,0:T(8,128)S(1)} %collective-permute-done.8.short_ref.refs_6_, ...), custom_call_target="tpu_custom_call" | custom-call | tf_op jit(solution)/shard_map/pack/pallas_call | solution.py:254
  64.0 5.4 %all-to-all-start = ((f32[32,8,256]{2,1,0:T(8,128)}), f32[32,8,256]{2,1,0:T(8,128)S(1)}, u32[]{:S(2)}, u32[]{:S(2)}) async-start(f32[32,8,256]{2,1,0:T(8,128)} %get-tuple-element.31), calls=%async_computation | async-start | bytes 524288 | tf_op jit(solution)/shard_map/all_to_all | solution.py:268
  69.4 9.6 %collective-permute-start.9 = (f32[4,7168]{1,0:T(4,128)S(1)}, f32[4,7168]{1,0:T(4,128)S(1)}, u32[]{:S(2)}, u32[]{:S(2)}) collective-permute-start(f32[4,7168]{1,0:T(4,128)S(1)} %get-tuple-element.32), channel_id=1, source_target_pairs={{0,32},{32,0},{64,96},{96,64},{128,160},{160,128},{192,224},{224,1... | collective-permute-start | bytes 344072 | tf_op jit(solution)/shard_map/ppermute | solution.py:267
  79.9 28.5 %all_to_all.15.mean_ref = f32[16,8,256]{2,1,0:T(8,128)S(1)} all-to-all(f32[16,8,256]{2,1,0:T(8,128)S(1)} %broadcast_in_dim.42), channel_id=1, replica_groups=mesh['fsdp'=16,'dp'=32] {'fsdp'}, dimensions={0} | all-to-all | bytes 262144 | tf_op jit(solution)/shard_map/all_to_all | solution.py:270
  108.5 4.8 %factor.1 = f32[32,8,384]{2,1,0:T(8,128)S(1)} custom-call(s32[4]{0:T(128)S(1)} %pad_add_fusion.where_ref, f32[16,8,256]{2,1,0:T(8,128)S(1)} %all_to_all.15.mean_ref), custom_call_target="tpu_custom_call" | custom-call | tf_op jit(solution)/shard_map/factor/pallas_call | solution.py:271
  113.3 18.1 %all_to_all.16.got_ref = f32[32,8,384]{2,1,0:T(8,128)S(1)} all-to-all(f32[32,8,384]{2,1,0:T(8,128)S(1)} %factor.1), channel_id=1, replica_groups=mesh['fsdp'=16,'dp'=32] {'dp'}, dimensions={0} | all-to-all | bytes 786432 | tf_op jit(solution)/shard_map/all_to_all | solution.py:279
  131.4 1.8 %unpack.1 = (f32[4,14336]{1,0:T(4,128)}, f32[4,448]{1,0:T(4,128)}, f32[32,896]{1,0:T(8,128)}) custom-call(s32[4]{0:T(128)S(1)} %pad_add_fusion.where_ref, f32[32,8,384]{2,1,0:T(8,128)S(1)} %all_to_all.16.got_ref, f32[4,7168]{1,0:T(4,128)S(1)} %get-tuple-element.34.kept_ref, f32[4,7168]{1,0:T(4,128)S(1)} %collective-permute-done.9.got_row_ref), custom_call_target="tpu_custom_call" | custom-call | tf_op jit(solution)/shard_map/unpack/pallas_call | solution.py:280
  (44 shorter events, 7.4 us)
Async XLA Ops:
  0.6 0.7 copy-start
  2.7 2.0 %copy-start.1 = (bf16[1,128,14336]{2,1,0:T(8,128)(2,1)S(1)}, bf16[1,128,14336]{2,1,0:T(8,128)(2,1)}, u32[]{:S(2)}) copy-start(bf16[1,128,14336]{2,1,0:T(8,128)(2,1)} %param.7) | copy-start | bytes 11010052
  4.8 12.3 %copy-start.2 = (bf16[1,128,14336]{2,1,0:T(8,128)(2,1)S(1)}, bf16[1,128,14336]{2,1,0:T(8,128)(2,1)}, u32[]{:S(2)}) copy-start(bf16[1,128,14336]{2,1,0:T(8,128)(2,1)} %param.7) | copy-start | bytes 11010052
  6.0 13.3 %copy-start.3 = (f32[896,32]{0,1:T(8,128)S(1)}, f32[896,32]{0,1:T(8,128)}, u32[]{:S(2)}) copy-start(f32[896,32]{0,1:T(8,128)} %param.9) | copy-start | bytes 344068
  6.0 12.3 %collective-permute-start = (f32[32,7168]{1,0:T(8,128)S(1)}, f32[32,7168]{1,0:T(8,128)S(1)}, u32[]{:S(2)}, u32[]{:S(2)}) collective-permute-start(f32[32,7168]{1,0:T(8,128)S(1)} %get-tuple-element.22), channel_id=1, source_target_pairs={{0,32},{32,0},{64,96},{96,64},{128,160},{160,128},{192,224},{224,1... | collective-permute-start | bytes 2752520 | tf_op jit(solution)/shard_map/ppermute | solution.py:234
  15.0 4.4 %collective-permute-start.5 = (f32[32,7168]{1,0:T(8,128)S(1)}, f32[32,7168]{1,0:T(8,128)S(1)}, u32[]{:S(2)}, u32[]{:S(2)}) collective-permute-start(f32[32,7168]{1,0:T(8,128)S(1)} %get-tuple-element.27), channel_id=1, source_target_pairs={{0,32},{32,0},{64,96},{96,64},{128,160},{160,128},{192,224},{224,1... | collective-permute-start | bytes 2752520 | tf_op jit(solution)/shard_map/ppermute | solution.py:235
  19.4 9.4 %collective-permute-start.1 = (f32[8,10752]{1,0:T(8,128)S(1)}, f32[8,10752]{1,0:T(8,128)S(1)}, u32[]{:S(2)}, u32[]{:S(2)}) collective-permute-start(f32[8,10752]{1,0:T(8,128)S(1)} %get-tuple-element.44), channel_id=1, source_target_pairs={{0,64},{64,128},{128,192},{192,256},{256,320},{320,384},{384,448},... | collective-permute-start | bytes 1032200 | tf_op jit(solution)/shard_map/ppermute | solution.py:242
  21.3 11.6 %collective-permute-start.6 = (f32[8,10752]{1,0:T(8,128)S(1)}, f32[8,10752]{1,0:T(8,128)S(1)}, u32[]{:S(2)}, u32[]{:S(2)}) collective-permute-start(f32[8,10752]{1,0:T(8,128)S(1)} %get-tuple-element.43), channel_id=1, source_target_pairs={{64,0},{128,64},{192,128},{256,192},{320,256},{384,320},{448,384},... | collective-permute-start | bytes 1032200 | tf_op jit(solution)/shard_map/ppermute | solution.py:251
  28.9 8.0 %collective-permute-start.2 = (f32[8,10752]{1,0:T(8,128)S(1)}, f32[8,10752]{1,0:T(8,128)S(1)}, u32[]{:S(2)}, u32[]{:S(2)}) collective-permute-start(f32[8,10752]{1,0:T(8,128)S(1)} %pad_maximum_fusion.2), channel_id=1, source_target_pairs={{0,64},{64,128},{128,192},{192,256},{256,320},{320,384},{384,448},... | collective-permute-start | bytes 1032200 | tf_op jit(solution)/shard_map/ppermute | solution.py:246
  33.0 20.4 %copy-start.4 = (s32[32]{0:T(128)S(1)}, s32[32]{0:T(128)}, u32[]{:S(2)}) copy-start(s32[32]{0:T(128)} %param.10) | copy-start | bytes 388
  33.0 20.4 %copy-start.5 = (s32[32]{0:T(128)S(1)}, s32[32]{0:T(128)}, u32[]{:S(2)}) copy-start(s32[32]{0:T(128)} %param.11) | copy-start | bytes 388
  33.0 12.7 %collective-permute-start.7 = (f32[8,10752]{1,0:T(8,128)S(1)}, f32[8,10752]{1,0:T(8,128)S(1)}, u32[]{:S(2)}, u32[]{:S(2)}) collective-permute-start(f32[8,10752]{1,0:T(8,128)S(1)} %pad_maximum_fusion.5), channel_id=1, source_target_pairs={{64,0},{128,64},{192,128},{256,192},{320,256},{384,320},{448,384},... | collective-permute-start | bytes 1032200 | tf_op jit(solution)/shard_map/ppermute | solution.py:251
  37.0 10.8 %collective-permute-start.3 = (f32[8,10752]{1,0:T(8,128)S(1)}, f32[8,10752]{1,0:T(8,128)S(1)}, u32[]{:S(2)}, u32[]{:S(2)}) collective-permute-start(f32[8,10752]{1,0:T(8,128)S(1)} %pad_maximum_fusion.3), channel_id=1, source_target_pairs={{0,64},{64,128},{128,192},{192,256},{256,320},{320,384},{384,448},... | collective-permute-start | bytes 1032200 | tf_op jit(solution)/shard_map/ppermute | solution.py:246
  45.8 12.4 %collective-permute-start.8 = (f32[8,10752]{1,0:T(8,128)S(1)}, f32[8,10752]{1,0:T(8,128)S(1)}, u32[]{:S(2)}, u32[]{:S(2)}) collective-permute-start(f32[8,10752]{1,0:T(8,128)S(1)} %pad_maximum_fusion.6), channel_id=1, source_target_pairs={{64,0},{128,64},{192,128},{256,192},{320,256},{384,320},{448,384},... | collective-permute-start | bytes 1032200 | tf_op jit(solution)/shard_map/ppermute | solution.py:251
  48.6 13.0 %collective-permute-start.4 = (f32[8,10752]{1,0:T(8,128)}, f32[8,10752]{1,0:T(8,128)S(1)}, u32[]{:S(2)}, u32[]{:S(2)}) collective-permute-start(f32[8,10752]{1,0:T(8,128)} %pad_maximum_fusion.4), channel_id=1, source_target_pairs={{0,64},{64,128},{128,192},{192,256},{256,320},{320,384},{384,448},... | collective-permute-start | bytes 1032200 | tf_op jit(solution)/shard_map/ppermute | solution.py:246
  64.0 15.8 %all-to-all-start = ((f32[32,8,256]{2,1,0:T(8,128)}), f32[32,8,256]{2,1,0:T(8,128)S(1)}, u32[]{:S(2)}, u32[]{:S(2)}) async-start(f32[32,8,256]{2,1,0:T(8,128)} %get-tuple-element.31), calls=%async_computation | async-start | bytes 524288 | tf_op jit(solution)/shard_map/all_to_all | solution.py:268
  69.4 10.5 %collective-permute-start.9 = (f32[4,7168]{1,0:T(4,128)S(1)}, f32[4,7168]{1,0:T(4,128)S(1)}, u32[]{:S(2)}, u32[]{:S(2)}) collective-permute-start(f32[4,7168]{1,0:T(4,128)S(1)} %get-tuple-element.32), channel_id=1, source_target_pairs={{0,32},{32,0},{64,96},{96,64},{128,160},{160,128},{192,224},{224,1... | collective-permute-start | bytes 344072 | tf_op jit(solution)/shard_map/ppermute | solution.py:267

commit v4 on v3

--- a/solution.py
+++ b/solution.py
@@ -47,6 +47,12 @@
                     out_refs[n][: size - chunk, cols] = out[first : first + size - chunk]
                 out_refs[n][size - chunk :, cols] = last
             first += size
+
+
+def step_kernel(came_ref, own_ref, got_ref, out_ref):
+    mid = own_ref.shape[1]
+    out_ref[:, :mid] = came_ref[:, :mid] + (own_ref[...] + got_ref[...])
+    out_ref[:, mid:] = came_ref[:, mid:]
 
 
 def pack_kernel(n_dp, piece, where_ref, mine_ref, long_ref, short_ref, own_ref, q_ref, *refs):
@@ -215,22 +221,22 @@
     place = jnp.arange(chunk)[:, None] // rows == core
     errors = jnp.where(place, jnp.concatenate([error_in[0], error_in[0]], axis=0), 0.0)
 
-    def product(side, splits):
+    def product(side, splits, limit):
         picked = (y + jnp.where(side == 0, ahead, -ahead)) % chips * chunk + jnp.arange(d_blk) % chunk
         onehot = (picked[:, None] == jnp.arange(d_blk)[None, :]).astype(a.dtype)
         chosen = jnp.einsum("nd,td->nt", onehot, a, preferred_element_type=F32).astype(a.dtype)
         return pl.pallas_call(
             functools.partial(product_kernel, splits),
-            out_shape=[jax.ShapeDtypeStruct((size, mid), F32) for size in splits],
+            out_shape=[pltpu.VMEM((size, mid), F32) for size in splits],
             in_specs=[SMEM, VMEM, pl.BlockSpec(memory_space=pl.ANY), VMEM],
             out_specs=[VMEM] * len(splits),
             scratch_shapes=[pltpu.VMEM((c.shape[0], mid), c.dtype), pltpu.SemaphoreType.DMA((chips,))],
-            compiler_params=pltpu.CompilerParams(vmem_limit_bytes=6 * 2**20),
+            compiler_params=pltpu.CompilerParams(vmem_limit_bytes=limit * 2**20),
             name="product",
         )(side[None], chosen, c, errors)
 
-    other_long, other_short = product(1 - core, (half * chunk, half * chunk))
-    far, *own = product(core, (chunk,) * chips)
+    other_long, other_short = product(1 - core, (half * chunk, half * chunk), 6)
+    far, *own = product(core, (chunk,) * chips, 6)
     got_long = lax.ppermute(other_long, "fsdp", swap)
     got_short = lax.ppermute(other_short, "fsdp", swap)
     far = far + got_long[:chunk]
@@ -243,7 +249,17 @@
     run_short = []
     for k in range(half - 1):
         last = run_long[-1]
-        run_long.append(lax.ppermute(jnp.concatenate([last[:, :mid] + long[k], last[:, mid:]], axis=1), "fsdp", rise))
+        start = jnp.concatenate([last[:, :mid] + long[k], last[:, mid:]], axis=1)
+        if k == half - 2:
+            start = pl.pallas_call(
+                step_kernel,
+                out_shape=pltpu.VMEM(start.shape, F32),
+                in_specs=[VMEM] * 3,
+                out_specs=VMEM,
+                compiler_params=pltpu.CompilerParams(vmem_limit_bytes=4 * 2**20),
+                name="step",
+            )(last, own[k], got_long[half * chunk - chunk :])
+        run_long.append(lax.ppermute(start, "fsdp", rise))
         if k == 0:
             last = jnp.concatenate([short[0], held], axis=1)
         else:

time: 134 us -> 133 us (level)
    ppermute x3, waiting for transfers between devices: 5.29 us -> 3.31 us  [shards(): run_long.append(lax.ppermute(start, 'fsdp', rise))]
  transfers between devices with their start and end apart: 11 -> 11, of which waited for: 9 -> 9; matrix products, arithmetic and copies ran while one was open for 2% -> 1% of each run, Pallas kernels for 1% -> 1%
where the time goes in v4:
time: 133 us; the launch traced here: 132 us
  blocking collectives  46.6 us (35%)
  starting transfers between devices  45.9 us (35%)
  waiting for transfers between devices  20.4 us (15%)
  Pallas kernels  11.7 us (9%)
  local copies, waits for them, and re-layouts  2.74 us (2%)
  other arithmetic  2.42 us (2%)
  between operations  2.27 us (2%)
    all_to_all x1, blocking collectives, shards(): lax.all_to_all(jnp.broadcast_to(mean[None], (groups, 8, width)), 'fsdp',...  28.5 us
    all_to_all x1, blocking collectives, shards(): got = lax.all_to_all(sent, 'dp', 0, 0, tiled=True)  18.1 us
    ppermute x3, waiting for transfers between devices, shards(): run_short.append(lax.ppermute(last, 'fsdp', fall))  11.1 us
    ppermute x3, starting transfers between devices, shards(): run_long.append(lax.ppermute(start, 'fsdp', rise))  9.87 us
    ppermute x1, starting transfers between devices, shards(): got_rows = lax.ppermute(given, 'fsdp', swap)  9.58 us
    ppermute x1, starting transfers between devices, shards(): got_long = lax.ppermute(other_long, 'fsdp', swap)  8.91 us
    ppermute x3, starting transfers between devices, shards(): run_short.append(lax.ppermute(last, 'fsdp', fall))  7.2 us
    all_to_all x1, starting transfers between devices, shards(): mean = jnp.sum(lax.all_to_all(sent, 'dp', 0, 0, tiled=True), axis=0)  6.45 us
  transfers between devices with their start and end apart: 11, of which 9 were waited for; matrix products, arithmetic and copies ran while one was open for 1% of the time, Pallas kernels for 1%

profile of v4, /device:TPU:1, one launch (start us, length us, event | category | flops | bytes accessed | tf_op | source)
XLA Modules:
  0.0 132.3 jit_solution(7234308212041494170)
XLA Ops:
  2.7 2.0 %copy-done.1 = bf16[1,128,14336]{2,1,0:T(8,128)(2,1)S(1)} copy-done((bf16[1,128,14336]{2,1,0:T(8,128)(2,1)S(1)}, bf16[1,128,14336]{2,1,0:T(8,128)(2,1)}, u32[]{:S(2)}) %copy-start.1) | copy-done | bytes 3670040
  6.0 8.9 %collective-permute-start = (f32[32,7168]{1,0:T(8,128)S(1)}, f32[32,7168]{1,0:T(8,128)S(1)}, u32[]{:S(2)}, u32[]{:S(2)}) collective-permute-start(f32[32,7168]{1,0:T(8,128)S(1)} %get-tuple-element.22), channel_id=1, source_target_pairs={{0,32},{32,0},{64,96},{96,64},{128,160},{160,128},{192,224},{224,1... | collective-permute-start | bytes 2752520 | tf_op jit(solution)/shard_map/ppermute | solution.py:240
  15.0 1.9 %collective-permute-start.5 = (f32[32,7168]{1,0:T(8,128)S(1)}, f32[32,7168]{1,0:T(8,128)S(1)}, u32[]{:S(2)}, u32[]{:S(2)}) collective-permute-start(f32[32,7168]{1,0:T(8,128)S(1)} %get-tuple-element.27), channel_id=1, source_target_pairs={{0,32},{32,0},{64,96},{96,64},{128,160},{160,128},{192,224},{224,1... | collective-permute-start | bytes 2752520 | tf_op jit(solution)/shard_map/ppermute | solution.py:241
  17.1 1.3 product.2
  19.4 1.9 %collective-permute-start.1 = (f32[8,10752]{1,0:T(8,128)S(1)}, f32[8,10752]{1,0:T(8,128)S(1)}, u32[]{:S(2)}, u32[]{:S(2)}) collective-permute-start(f32[8,10752]{1,0:T(8,128)S(1)} %get-tuple-element.46), channel_id=1, source_target_pairs={{0,64},{64,128},{128,192},{192,256},{256,320},{320,384},{384,448},... | collective-permute-start | bytes 1032200 | tf_op jit(solution)/shard_map/ppermute | solution.py:248
  21.3 3.4 %collective-permute-start.6 = (f32[8,10752]{1,0:T(8,128)S(1)}, f32[8,10752]{1,0:T(8,128)S(1)}, u32[]{:S(2)}, u32[]{:S(2)}) collective-permute-start(f32[8,10752]{1,0:T(8,128)S(1)} %get-tuple-element.45), channel_id=1, source_target_pairs={{64,0},{128,64},{192,128},{256,192},{320,256},{384,320},{448,384},... | collective-permute-start | bytes 1032200 | tf_op jit(solution)/shard_map/ppermute | solution.py:267
  24.7 4.1 %collective-permute-done.1.refs_0_ = f32[8,10752]{1,0:T(8,128)S(1)} collective-permute-done((f32[8,10752]{1,0:T(8,128)S(1)}, f32[8,10752]{1,0:T(8,128)S(1)}, u32[]{:S(2)}, u32[]{:S(2)}) %collective-permute-start.1) | collective-permute-done | bytes 344096 | tf_op jit(solution)/shard_map/ppermute | solution.py:248
  28.9 1.9 %collective-permute-start.2 = (f32[8,10752]{1,0:T(8,128)S(1)}, f32[8,10752]{1,0:T(8,128)S(1)}, u32[]{:S(2)}, u32[]{:S(2)}) collective-permute-start(f32[8,10752]{1,0:T(8,128)S(1)} %pad_maximum_fusion.2), channel_id=1, source_target_pairs={{0,64},{64,128},{128,192},{192,256},{256,320},{320,384},{384,448},... | collective-permute-start | bytes 1032200 | tf_op jit(solution)/shard_map/ppermute | solution.py:262
  30.8 2.1 %collective-permute-done.6.refs_4_ = f32[8,10752]{1,0:T(8,128)S(1)} collective-permute-done((f32[8,10752]{1,0:T(8,128)S(1)}, f32[8,10752]{1,0:T(8,128)S(1)}, u32[]{:S(2)}, u32[]{:S(2)}) %collective-permute-start.6) | collective-permute-done | bytes 344096 | tf_op jit(solution)/shard_map/ppermute | solution.py:267
  33.0 1.9 %collective-permute-start.7 = (f32[8,10752]{1,0:T(8,128)S(1)}, f32[8,10752]{1,0:T(8,128)S(1)}, u32[]{:S(2)}, u32[]{:S(2)}) collective-permute-start(f32[8,10752]{1,0:T(8,128)S(1)} %pad_maximum_fusion.4), channel_id=1, source_target_pairs={{64,0},{128,64},{192,128},{256,192},{320,256},{384,320},{448,384},... | collective-permute-start | bytes 1032200 | tf_op jit(solution)/shard_map/ppermute | solution.py:267
  34.9 1.9 %collective-permute-done.2.refs_1_ = f32[8,10752]{1,0:T(8,128)S(1)} collective-permute-done((f32[8,10752]{1,0:T(8,128)S(1)}, f32[8,10752]{1,0:T(8,128)S(1)}, u32[]{:S(2)}, u32[]{:S(2)}) %collective-permute-start.2) | collective-permute-done | bytes 344096 | tf_op jit(solution)/shard_map/ppermute | solution.py:262
  37.0 3.1 %collective-permute-start.3 = (f32[8,10752]{1,0:T(8,128)S(1)}, f32[8,10752]{1,0:T(8,128)S(1)}, u32[]{:S(2)}, u32[]{:S(2)}) collective-permute-start(f32[8,10752]{1,0:T(8,128)S(1)} %pad_maximum_fusion.3), channel_id=1, source_target_pairs={{0,64},{64,128},{128,192},{192,256},{256,320},{320,384},{384,448},... | collective-permute-start | bytes 1032200 | tf_op jit(solution)/shard_map/ppermute | solution.py:262
  40.1 5.6 %collective-permute-done.7.refs_5_ = f32[8,10752]{1,0:T(8,128)S(1)} collective-permute-done((f32[8,10752]{1,0:T(8,128)S(1)}, f32[8,10752]{1,0:T(8,128)S(1)}, u32[]{:S(2)}, u32[]{:S(2)}) %collective-permute-start.7) | collective-permute-done | bytes 344096 | tf_op jit(solution)/shard_map/ppermute | solution.py:267
  45.8 1.9 %collective-permute-start.8 = (f32[8,10752]{1,0:T(8,128)S(1)}, f32[8,10752]{1,0:T(8,128)S(1)}, u32[]{:S(2)}, u32[]{:S(2)}) collective-permute-start(f32[8,10752]{1,0:T(8,128)S(1)} %pad_maximum_fusion.5), channel_id=1, source_target_pairs={{64,0},{128,64},{192,128},{256,192},{320,256},{384,320},{448,384},... | collective-permute-start | bytes 1032200 | tf_op jit(solution)/shard_map/ppermute | solution.py:267
  47.8 4.8 %collective-permute-start.4 = (f32[8,10752]{1,0:T(8,128)S(1)}, f32[8,10752]{1,0:T(8,128)S(1)}, u32[]{:S(2)}, u32[]{:S(2)}) collective-permute-start(f32[8,10752]{1,0:T(8,128)S(1)} %step.1), channel_id=1, source_target_pairs={{0,64},{64,128},{128,192},{192,256},{256,320},{320,384},{384,448},... | collective-permute-start | bytes 1032200 | tf_op jit(solution)/shard_map/ppermute | solution.py:262
  54.7 3.5 %collective-permute-done.8.short_ref.refs_6_ = f32[8,10752]{1,0:T(8,128)S(1)} collective-permute-done((f32[8,10752]{1,0:T(8,128)S(1)}, f32[8,10752]{1,0:T(8,128)S(1)}, u32[]{:S(2)}, u32[]{:S(2)}) %collective-permute-start.8) | collective-permute-done | bytes 344096 | tf_op jit(solution)/shard_map/ppermute | solution.py:267
  58.2 1.4 %collective-permute-done.4.long_ref.refs_3_ = f32[8,10752]{1,0:T(8,128)S(1)} collective-permute-done((f32[8,10752]{1,0:T(8,128)S(1)}, f32[8,10752]{1,0:T(8,128)S(1)}, u32[]{:S(2)}, u32[]{:S(2)}) %collective-permute-start.4) | collective-permute-done | bytes 344096 | tf_op jit(solution)/shard_map/ppermute | solution.py:262
  59.6 2.4 %pack.1 = (f32[32,8,256]{2,1,0:T(8,128)}, f32[4,7168]{1,0:T(4,128)S(1)}, f32[4,7168]{1,0:T(4,128)S(1)}) custom-call(s32[4]{0:T(128)S(1)} %pad_add_fusion.where_ref, f32[1]{0:T(128)} %bitcast.4.mine_ref, f32[8,10752]{1,0:T(8,128)S(1)} %collective-permute-done.4.long_ref.refs_3_, f32[8,10752]{1,0:T(8,128)S(1)} %collective-permute-done.8.short_ref.refs_6_, ...), custom_call_target="tpu_custom_call" | custom-call | tf_op jit(solution)/shard_map/pack/pallas_call | solution.py:270
  62.0 6.4 %all-to-all-start = ((f32[32,8,256]{2,1,0:T(8,128)}), f32[32,8,256]{2,1,0:T(8,128)S(1)}, u32[]{:S(2)}, u32[]{:S(2)}) async-start(f32[32,8,256]{2,1,0:T(8,128)} %get-tuple-element.31), calls=%async_computation | async-start | bytes 524288 | tf_op jit(solution)/shard_map/all_to_all | solution.py:284
  68.5 9.6 %collective-permute-start.9 = (f32[4,7168]{1,0:T(4,128)S(1)}, f32[4,7168]{1,0:T(4,128)S(1)}, u32[]{:S(2)}, u32[]{:S(2)}) collective-permute-start(f32[4,7168]{1,0:T(4,128)S(1)} %get-tuple-element.32), channel_id=1, source_target_pairs={{0,32},{32,0},{64,96},{96,64},{128,160},{160,128},{192,224},{224,1... | collective-permute-start | bytes 344072 | tf_op jit(solution)/shard_map/ppermute | solution.py:283
  79.0 28.5 %all_to_all.15.mean_ref = f32[16,8,256]{2,1,0:T(8,128)S(1)} all-to-all(f32[16,8,256]{2,1,0:T(8,128)S(1)} %broadcast_in_dim.42), channel_id=1, replica_groups=mesh['fsdp'=16,'dp'=32] {'fsdp'}, dimensions={0} | all-to-all | bytes 262144 | tf_op jit(solution)/shard_map/all_to_all | solution.py:286
  107.5 4.8 %factor.1 = f32[32,8,384]{2,1,0:T(8,128)S(1)} custom-call(s32[4]{0:T(128)S(1)} %pad_add_fusion.where_ref, f32[16,8,256]{2,1,0:T(8,128)S(1)} %all_to_all.15.mean_ref), custom_call_target="tpu_custom_call" | custom-call | tf_op jit(solution)/shard_map/factor/pallas_call | solution.py:287
  112.4 18.1 %all_to_all.16.got_ref = f32[32,8,384]{2,1,0:T(8,128)S(1)} all-to-all(f32[32,8,384]{2,1,0:T(8,128)S(1)} %factor.1), channel_id=1, replica_groups=mesh['fsdp'=16,'dp'=32] {'dp'}, dimensions={0} | all-to-all | bytes 786432 | tf_op jit(solution)/shard_map/all_to_all | solution.py:295
  130.5 1.8 %unpack.1 = (f32[4,14336]{1,0:T(4,128)}, f32[4,448]{1,0:T(4,128)}, f32[32,896]{1,0:T(8,128)}) custom-call(s32[4]{0:T(128)S(1)} %pad_add_fusion.where_ref, f32[32,8,384]{2,1,0:T(8,128)S(1)} %all_to_all.16.got_ref, f32[4,7168]{1,0:T(4,128)S(1)} %get-tuple-element.34.kept_ref, f32[4,7168]{1,0:T(4,128)S(1)} %collective-permute-done.9.got_row_ref), custom_call_target="tpu_custom_call" | custom-call | tf_op jit(solution)/shard_map/unpack/pallas_call | solution.py:296
  (42 shorter events, 6.7 us)
Async XLA Ops:
  0.6 0.7 copy-start
  2.7 2.0 %copy-start.1 = (bf16[1,128,14336]{2,1,0:T(8,128)(2,1)S(1)}, bf16[1,128,14336]{2,1,0:T(8,128)(2,1)}, u32[]{:S(2)}) copy-start(bf16[1,128,14336]{2,1,0:T(8,128)(2,1)} %param.7) | copy-start | bytes 11010052
  4.8 12.3 %copy-start.2 = (bf16[1,128,14336]{2,1,0:T(8,128)(2,1)S(1)}, bf16[1,128,14336]{2,1,0:T(8,128)(2,1)}, u32[]{:S(2)}) copy-start(bf16[1,128,14336]{2,1,0:T(8,128)(2,1)} %param.7) | copy-start | bytes 11010052
  6.0 13.3 %copy-start.3 = (f32[896,32]{0,1:T(8,128)S(1)}, f32[896,32]{0,1:T(8,128)}, u32[]{:S(2)}) copy-start(f32[896,32]{0,1:T(8,128)} %param.9) | copy-start | bytes 344068
  6.0 12.3 %collective-permute-start = (f32[32,7168]{1,0:T(8,128)S(1)}, f32[32,7168]{1,0:T(8,128)S(1)}, u32[]{:S(2)}, u32[]{:S(2)}) collective-permute-start(f32[32,7168]{1,0:T(8,128)S(1)} %get-tuple-element.22), channel_id=1, source_target_pairs={{0,32},{32,0},{64,96},{96,64},{128,160},{160,128},{192,224},{224,1... | collective-permute-start | bytes 2752520 | tf_op jit(solution)/shard_map/ppermute | solution.py:240
  15.0 4.4 %collective-permute-start.5 = (f32[32,7168]{1,0:T(8,128)S(1)}, f32[32,7168]{1,0:T(8,128)S(1)}, u32[]{:S(2)}, u32[]{:S(2)}) collective-permute-start(f32[32,7168]{1,0:T(8,128)S(1)} %get-tuple-element.27), channel_id=1, source_target_pairs={{0,32},{32,0},{64,96},{96,64},{128,160},{160,128},{192,224},{224,1... | collective-permute-start | bytes 2752520 | tf_op jit(solution)/shard_map/ppermute | solution.py:241
  19.4 9.4 %collective-permute-start.1 = (f32[8,10752]{1,0:T(8,128)S(1)}, f32[8,10752]{1,0:T(8,128)S(1)}, u32[]{:S(2)}, u32[]{:S(2)}) collective-permute-start(f32[8,10752]{1,0:T(8,128)S(1)} %get-tuple-element.46), channel_id=1, source_target_pairs={{0,64},{64,128},{128,192},{192,256},{256,320},{320,384},{384,448},... | collective-permute-start | bytes 1032200 | tf_op jit(solution)/shard_map/ppermute | solution.py:248
  21.3 11.6 %collective-permute-start.6 = (f32[8,10752]{1,0:T(8,128)S(1)}, f32[8,10752]{1,0:T(8,128)S(1)}, u32[]{:S(2)}, u32[]{:S(2)}) collective-permute-start(f32[8,10752]{1,0:T(8,128)S(1)} %get-tuple-element.45), channel_id=1, source_target_pairs={{64,0},{128,64},{192,128},{256,192},{320,256},{384,320},{448,384},... | collective-permute-start | bytes 1032200 | tf_op jit(solution)/shard_map/ppermute | solution.py:267
  28.9 8.0 %collective-permute-start.2 = (f32[8,10752]{1,0:T(8,128)S(1)}, f32[8,10752]{1,0:T(8,128)S(1)}, u32[]{:S(2)}, u32[]{:S(2)}) collective-permute-start(f32[8,10752]{1,0:T(8,128)S(1)} %pad_maximum_fusion.2), channel_id=1, source_target_pairs={{0,64},{64,128},{128,192},{192,256},{256,320},{320,384},{384,448},... | collective-permute-start | bytes 1032200 | tf_op jit(solution)/shard_map/ppermute | solution.py:262
  32.9 19.7 %copy-start.4 = (s32[32]{0:T(128)S(1)}, s32[32]{0:T(128)}, u32[]{:S(2)}) copy-start(s32[32]{0:T(128)} %param.10) | copy-start | bytes 388
  32.9 19.7 %copy-start.5 = (s32[32]{0:T(128)S(1)}, s32[32]{0:T(128)}, u32[]{:S(2)}) copy-start(s32[32]{0:T(128)} %param.11) | copy-start | bytes 388
  33.0 12.7 %collective-permute-start.7 = (f32[8,10752]{1,0:T(8,128)S(1)}, f32[8,10752]{1,0:T(8,128)S(1)}, u32[]{:S(2)}, u32[]{:S(2)}) collective-permute-start(f32[8,10752]{1,0:T(8,128)S(1)} %pad_maximum_fusion.4), channel_id=1, source_target_pairs={{64,0},{128,64},{192,128},{256,192},{320,256},{384,320},{448,384},... | collective-permute-start | bytes 1032200 | tf_op jit(solution)/shard_map/ppermute | solution.py:267
  37.0 10.8 %collective-permute-start.3 = (f32[8,10752]{1,0:T(8,128)S(1)}, f32[8,10752]{1,0:T(8,128)S(1)}, u32[]{:S(2)}, u32[]{:S(2)}) collective-permute-start(f32[8,10752]{1,0:T(8,128)S(1)} %pad_maximum_fusion.3), channel_id=1, source_target_pairs={{0,64},{64,128},{128,192},{192,256},{256,320},{320,384},{384,448},... | collective-permute-start | bytes 1032200 | tf_op jit(solution)/shard_map/ppermute | solution.py:262
  45.8 12.4 %collective-permute-start.8 = (f32[8,10752]{1,0:T(8,128)S(1)}, f32[8,10752]{1,0:T(8,128)S(1)}, u32[]{:S(2)}, u32[]{:S(2)}) collective-permute-start(f32[8,10752]{1,0:T(8,128)S(1)} %pad_maximum_fusion.5), channel_id=1, source_target_pairs={{64,0},{128,64},{192,128},{256,192},{320,256},{384,320},{448,384},... | collective-permute-start | bytes 1032200 | tf_op jit(solution)/shard_map/ppermute | solution.py:267
  47.8 11.7 %collective-permute-start.4 = (f32[8,10752]{1,0:T(8,128)S(1)}, f32[8,10752]{1,0:T(8,128)S(1)}, u32[]{:S(2)}, u32[]{:S(2)}) collective-permute-start(f32[8,10752]{1,0:T(8,128)S(1)} %step.1), channel_id=1, source_target_pairs={{0,64},{64,128},{128,192},{192,256},{256,320},{320,384},{384,448},... | collective-permute-start | bytes 1032200 | tf_op jit(solution)/shard_map/ppermute | solution.py:262
  62.0 16.9 %all-to-all-start = ((f32[32,8,256]{2,1,0:T(8,128)}), f32[32,8,256]{2,1,0:T(8,128)S(1)}, u32[]{:S(2)}, u32[]{:S(2)}) async-start(f32[32,8,256]{2,1,0:T(8,128)} %get-tuple-element.31), calls=%async_computation | async-start | bytes 524288 | tf_op jit(solution)/shard_map/all_to_all | solution.py:284
  68.5 10.5 %collective-permute-start.9 = (f32[4,7168]{1,0:T(4,128)S(1)}, f32[4,7168]{1,0:T(4,128)S(1)}, u32[]{:S(2)}, u32[]{:S(2)}) collective-permute-start(f32[4,7168]{1,0:T(4,128)S(1)} %get-tuple-element.32), channel_id=1, source_target_pairs={{0,32},{32,0},{64,96},{96,64},{128,160},{160,128},{192,224},{224,1... | collective-permute-start | bytes 344072 | tf_op jit(solution)/shard_map/ppermute | solution.py:283

commit v5 on v4

--- a/solution.py
+++ b/solution.py
@@ -75,7 +75,7 @@
             held = shard_refs[k - 1][:, mid:]
             shard = jnp.concatenate([held[:, a * span : (a + 1) * span] for a in range(rank // 8)], axis=0)
             step = k if k <= chips // 2 else chips // 2 - k
-            chip = lax.rem(y + chips - jnp.where(core == 0, step, -step), chips)
+            chip = lax.rem(y + chips - jnp.where(core == 0, -step, step), chips)
         start = pl.multiple_of(chip * span, LANES)
         parts = parts + contract(sum_ref[:, pl.ds(start, span)], shard, (1, 1))
 
@@ -212,7 +212,7 @@
     mine = jnp.sum(jnp.where(jnp.arange(islands) == i, weight, 0.0)) / total
 
     swap = [(k, k ^ 1) for k in range(groups)]
-    rise = [(2 * k, 2 * ((k + 1) % chips)) for k in range(chips)] + [(2 * k + 1, 2 * ((k - 1) % chips) + 1) for k in range(chips)]
+    rise = [(2 * k, 2 * ((k - 1) % chips)) for k in range(chips)] + [(2 * k + 1, 2 * ((k + 1) % chips) + 1) for k in range(chips)]
     fall = [(k, j) for j, k in rise]
     where = jnp.stack([y, core, i, f])
     block = jnp.arange(d_blk) // chunk
@@ -222,7 +222,7 @@
     errors = jnp.where(place, jnp.concatenate([error_in[0], error_in[0]], axis=0), 0.0)
 
     def product(side, splits, limit):
-        picked = (y + jnp.where(side == 0, ahead, -ahead)) % chips * chunk + jnp.arange(d_blk) % chunk
+        picked = (y + jnp.where(side == 0, -ahead, ahead)) % chips * chunk + jnp.arange(d_blk) % chunk
         onehot = (picked[:, None] == jnp.arange(d_blk)[None, :]).astype(a.dtype)
         chosen = jnp.einsum("nd,td->nt", onehot, a, preferred_element_type=F32).astype(a.dtype)
         return pl.pallas_call(

time: 133 us -> 131 us (0.985)
  blocking collectives: 46.6 us -> 39.5 us
  starting transfers between devices: 45.9 us -> 51.1 us
    ppermute x3, waiting for transfers between devices: 11.1 us -> 3.41 us  [shards(): run_short.append(lax.ppermute(last, 'fsdp', fall))]
    all_to_all x1, blocking collectives: 28.5 us -> 21.4 us  [shards(): lax.all_to_all(jnp.broadcast_to(mean[None], (groups, 8, width)), 'fsdp',...]
    ppermute x3, waiting for transfers between devices: 3.31 us -> 9.5 us  [shards(): run_long.append(lax.ppermute(start, 'fsdp', rise))]
    all_to_all x1, starting transfers between devices: 6.45 us -> 12.2 us  [shards(): mean = jnp.sum(lax.all_to_all(sent, 'dp', 0, 0, tiled=True), axis=0)]
    ppermute x3, starting transfers between devices: 7.2 us -> 12.2 us  [shards(): run_short.append(lax.ppermute(last, 'fsdp', fall))]
    ppermute x3, starting transfers between devices: 9.87 us -> 5.76 us  [shards(): run_long.append(lax.ppermute(start, 'fsdp', rise))]
    all_to_all x1, waiting for transfers between devices: 0.81 us -> 2.2 us  [shards(): mean = jnp.sum(lax.all_to_all(sent, 'dp', 0, 0, tiled=True), axis=0)]
    ppermute x1, starting transfers between devices: 9.58 us -> 8.23 us  [shards(): got_rows = lax.ppermute(given, 'fsdp', swap)]
  transfers between devices with their start and end apart: 11 -> 11, of which waited for: 9 -> 8; matrix products, arithmetic and copies ran while one was open for 1% -> 1% of each run, Pallas kernels for 1% -> 1%
where the time goes in v5:
time: 131 us; the launch traced here: 130 us
  starting transfers between devices  51.1 us (39%)
  blocking collectives  39.5 us (30%)
  waiting for transfers between devices  20.1 us (15%)
  Pallas kernels  11.6 us (9%)
  local copies, waits for them, and re-layouts  2.74 us (2%)
  other arithmetic  2.42 us (2%)
  between operations  2.28 us (2%)
    all_to_all x1, blocking collectives, shards(): lax.all_to_all(jnp.broadcast_to(mean[None], (groups, 8, width)), 'fsdp',...  21.4 us
    all_to_all x1, blocking collectives, shards(): got = lax.all_to_all(sent, 'dp', 0, 0, tiled=True)  18.1 us
    ppermute x3, starting transfers between devices, shards(): run_short.append(lax.ppermute(last, 'fsdp', fall))  12.2 us
    all_to_all x1, starting transfers between devices, shards(): mean = jnp.sum(lax.all_to_all(sent, 'dp', 0, 0, tiled=True), axis=0)  12.2 us
    ppermute x3, waiting for transfers between devices, shards(): run_long.append(lax.ppermute(start, 'fsdp', rise))  9.5 us
    ppermute x1, starting transfers between devices, shards(): got_long = lax.ppermute(other_long, 'fsdp', swap)  8.91 us
    ppermute x1, starting transfers between devices, shards(): got_rows = lax.ppermute(given, 'fsdp', swap)  8.23 us
    ppermute x3, starting transfers between devices, shards(): run_long.append(lax.ppermute(start, 'fsdp', rise))  5.76 us
  transfers between devices with their start and end apart: 11, of which 8 were waited for; matrix products, arithmetic and copies ran while one was open for 1% of the time, Pallas kernels for 1%

profile of v5, /device:TPU:1, one launch (start us, length us, event | category | flops | bytes accessed | tf_op | source)
XLA Modules:
  0.0 130.2 jit_solution(13666498947261581657)
XLA Ops:
  2.7 2.0 %copy-done.1 = bf16[1,128,14336]{2,1,0:T(8,128)(2,1)S(1)} copy-done((bf16[1,128,14336]{2,1,0:T(8,128)(2,1)S(1)}, bf16[1,128,14336]{2,1,0:T(8,128)(2,1)}, u32[]{:S(2)}) %copy-start.1) | copy-done | bytes 3670040
  6.0 8.9 %collective-permute-start = (f32[32,7168]{1,0:T(8,128)S(1)}, f32[32,7168]{1,0:T(8,128)S(1)}, u32[]{:S(2)}, u32[]{:S(2)}) collective-permute-start(f32[32,7168]{1,0:T(8,128)S(1)} %get-tuple-element.22), channel_id=1, source_target_pairs={{0,32},{32,0},{64,96},{96,64},{128,160},{160,128},{192,224},{224,1... | collective-permute-start | bytes 2752520 | tf_op jit(solution)/shard_map/ppermute | solution.py:240
  15.0 1.9 %collective-permute-start.5 = (f32[32,7168]{1,0:T(8,128)S(1)}, f32[32,7168]{1,0:T(8,128)S(1)}, u32[]{:S(2)}, u32[]{:S(2)}) collective-permute-start(f32[32,7168]{1,0:T(8,128)S(1)} %get-tuple-element.27), channel_id=1, source_target_pairs={{0,32},{32,0},{64,96},{96,64},{128,160},{160,128},{192,224},{224,1... | collective-permute-start | bytes 2752520 | tf_op jit(solution)/shard_map/ppermute | solution.py:241
  19.4 1.9 %collective-permute-start.1 = (f32[8,10752]{1,0:T(8,128)S(1)}, f32[8,10752]{1,0:T(8,128)S(1)}, u32[]{:S(2)}, u32[]{:S(2)}) collective-permute-start(f32[8,10752]{1,0:T(8,128)S(1)} %get-tuple-element.46), channel_id=1, source_target_pairs={{0,448},{64,0},{128,64},{192,128},{256,192},{320,256},{384,320},{4... | collective-permute-start | bytes 1032200 | tf_op jit(solution)/shard_map/ppermute | solution.py:248
  21.3 4.6 %collective-permute-start.6 = (f32[8,10752]{1,0:T(8,128)S(1)}, f32[8,10752]{1,0:T(8,128)S(1)}, u32[]{:S(2)}, u32[]{:S(2)}) collective-permute-start(f32[8,10752]{1,0:T(8,128)S(1)} %get-tuple-element.45), channel_id=1, source_target_pairs={{448,0},{0,64},{64,128},{128,192},{192,256},{256,320},{320,384},{3... | collective-permute-start | bytes 1032200 | tf_op jit(solution)/shard_map/ppermute | solution.py:267
  25.9 4.1 %collective-permute-done.1.refs_0_ = f32[8,10752]{1,0:T(8,128)S(1)} collective-permute-done((f32[8,10752]{1,0:T(8,128)S(1)}, f32[8,10752]{1,0:T(8,128)S(1)}, u32[]{:S(2)}, u32[]{:S(2)}) %collective-permute-start.1) | collective-permute-done | bytes 344096 | tf_op jit(solution)/shard_map/ppermute | solution.py:248
  30.1 1.9 %collective-permute-start.2 = (f32[8,10752]{1,0:T(8,128)S(1)}, f32[8,10752]{1,0:T(8,128)S(1)}, u32[]{:S(2)}, u32[]{:S(2)}) collective-permute-start(f32[8,10752]{1,0:T(8,128)S(1)} %pad_maximum_fusion.2), channel_id=1, source_target_pairs={{0,448},{64,0},{128,64},{192,128},{256,192},{320,256},{384,320},{4... | collective-permute-start | bytes 1032200 | tf_op jit(solution)/shard_map/ppermute | solution.py:262
  32.2 4.6 %collective-permute-start.7 = (f32[8,10752]{1,0:T(8,128)S(1)}, f32[8,10752]{1,0:T(8,128)S(1)}, u32[]{:S(2)}, u32[]{:S(2)}) collective-permute-start(f32[8,10752]{1,0:T(8,128)S(1)} %pad_maximum_fusion.4), channel_id=1, source_target_pairs={{448,0},{0,64},{64,128},{128,192},{192,256},{256,320},{320,384},{3... | collective-permute-start | bytes 1032200 | tf_op jit(solution)/shard_map/ppermute | solution.py:267
  36.7 3.0 %collective-permute-done.2.refs_1_ = f32[8,10752]{1,0:T(8,128)S(1)} collective-permute-done((f32[8,10752]{1,0:T(8,128)S(1)}, f32[8,10752]{1,0:T(8,128)S(1)}, u32[]{:S(2)}, u32[]{:S(2)}) %collective-permute-start.2) | collective-permute-done | bytes 344096 | tf_op jit(solution)/shard_map/ppermute | solution.py:262
  39.8 1.9 %collective-permute-start.3 = (f32[8,10752]{1,0:T(8,128)S(1)}, f32[8,10752]{1,0:T(8,128)S(1)}, u32[]{:S(2)}, u32[]{:S(2)}) collective-permute-start(f32[8,10752]{1,0:T(8,128)S(1)} %pad_maximum_fusion.3), channel_id=1, source_target_pairs={{0,448},{64,0},{128,64},{192,128},{256,192},{320,256},{384,320},{4... | collective-permute-start | bytes 1032200 | tf_op jit(solution)/shard_map/ppermute | solution.py:262
  41.7 1.6 %collective-permute-done.7.refs_5_ = f32[8,10752]{1,0:T(8,128)S(1)} collective-permute-done((f32[8,10752]{1,0:T(8,128)S(1)}, f32[8,10752]{1,0:T(8,128)S(1)}, u32[]{:S(2)}, u32[]{:S(2)}) %collective-permute-start.7) | collective-permute-done | bytes 344096 | tf_op jit(solution)/shard_map/ppermute | solution.py:267
  43.4 3.0 %collective-permute-start.8 = (f32[8,10752]{1,0:T(8,128)S(1)}, f32[8,10752]{1,0:T(8,128)S(1)}, u32[]{:S(2)}, u32[]{:S(2)}) collective-permute-start(f32[8,10752]{1,0:T(8,128)S(1)} %pad_maximum_fusion.5), channel_id=1, source_target_pairs={{448,0},{0,64},{64,128},{128,192},{192,256},{256,320},{320,384},{3... | collective-permute-start | bytes 1032200 | tf_op jit(solution)/shard_map/ppermute | solution.py:267
  46.4 2.6 %collective-permute-done.3.came_ref.refs_2_ = f32[8,10752]{1,0:T(8,128)S(1)} collective-permute-done((f32[8,10752]{1,0:T(8,128)S(1)}, f32[8,10752]{1,0:T(8,128)S(1)}, u32[]{:S(2)}, u32[]{:S(2)}) %collective-permute-start.3) | collective-permute-done | bytes 344096 | tf_op jit(solution)/shard_map/ppermute | solution.py:262
  49.1 1.9 %collective-permute-start.4 = (f32[8,10752]{1,0:T(8,128)S(1)}, f32[8,10752]{1,0:T(8,128)S(1)}, u32[]{:S(2)}, u32[]{:S(2)}) collective-permute-start(f32[8,10752]{1,0:T(8,128)S(1)} %step.1), channel_id=1, source_target_pairs={{0,448},{64,0},{128,64},{192,128},{256,192},{320,256},{384,320},{4... | collective-permute-start | bytes 1032200 | tf_op jit(solution)/shard_map/ppermute | solution.py:262
  53.1 1.8 %collective-permute-done.8.short_ref.refs_6_ = f32[8,10752]{1,0:T(8,128)S(1)} collective-permute-done((f32[8,10752]{1,0:T(8,128)S(1)}, f32[8,10752]{1,0:T(8,128)S(1)}, u32[]{:S(2)}, u32[]{:S(2)}) %collective-permute-start.8) | collective-permute-done | bytes 344096 | tf_op jit(solution)/shard_map/ppermute | solution.py:267
  54.9 4.0 %collective-permute-done.4.long_ref.refs_3_ = f32[8,10752]{1,0:T(8,128)S(1)} collective-permute-done((f32[8,10752]{1,0:T(8,128)S(1)}, f32[8,10752]{1,0:T(8,128)S(1)}, u32[]{:S(2)}, u32[]{:S(2)}) %collective-permute-start.4) | collective-permute-done | bytes 344096 | tf_op jit(solution)/shard_map/ppermute | solution.py:262
  58.9 2.4 %pack.1 = (f32[32,8,256]{2,1,0:T(8,128)}, f32[4,7168]{1,0:T(4,128)S(1)}, f32[4,7168]{1,0:T(4,128)S(1)}) custom-call(s32[4]{0:T(128)S(1)} %pad_add_fusion.where_ref, f32[1]{0:T(128)} %bitcast.4.mine_ref, f32[8,10752]{1,0:T(8,128)S(1)} %collective-permute-done.4.long_ref.refs_3_, f32[8,10752]{1,0:T(8,128)S(1)} %collective-permute-done.8.short_ref.refs_6_, ...), custom_call_target="tpu_custom_call" | custom-call | tf_op jit(solution)/shard_map/pack/pallas_call | solution.py:270
  61.3 12.2 %all-to-all-start = ((f32[32,8,256]{2,1,0:T(8,128)}), f32[32,8,256]{2,1,0:T(8,128)S(1)}, u32[]{:S(2)}, u32[]{:S(2)}) async-start(f32[32,8,256]{2,1,0:T(8,128)} %get-tuple-element.31), calls=%async_computation | async-start | bytes 524288 | tf_op jit(solution)/shard_map/all_to_all | solution.py:284
  73.5 8.2 %collective-permute-start.9 = (f32[4,7168]{1,0:T(4,128)S(1)}, f32[4,7168]{1,0:T(4,128)S(1)}, u32[]{:S(2)}, u32[]{:S(2)}) collective-permute-start(f32[4,7168]{1,0:T(4,128)S(1)} %get-tuple-element.32), channel_id=1, source_target_pairs={{0,32},{32,0},{64,96},{96,64},{128,160},{160,128},{192,224},{224,1... | collective-permute-start | bytes 344072 | tf_op jit(solution)/shard_map/ppermute | solution.py:283
  81.8 2.2 %all-to-all-done = f32[32,8,256]{2,1,0:T(8,128)S(1)} async-done(((f32[32,8,256]{2,1,0:T(8,128)}), f32[32,8,256]{2,1,0:T(8,128)S(1)}, u32[]{:S(2)}, u32[]{:S(2)}) %all-to-all-start) | async-done | bytes 262176 | tf_op jit(solution)/shard_map/all_to_all | solution.py:284
  84.0 21.4 %all_to_all.15.mean_ref = f32[16,8,256]{2,1,0:T(8,128)S(1)} all-to-all(f32[16,8,256]{2,1,0:T(8,128)S(1)} %broadcast_in_dim.42), channel_id=1, replica_groups=mesh['fsdp'=16,'dp'=32] {'fsdp'}, dimensions={0} | all-to-all | bytes 262144 | tf_op jit(solution)/shard_map/all_to_all | solution.py:286
  105.4 4.8 %factor.1 = f32[32,8,384]{2,1,0:T(8,128)S(1)} custom-call(s32[4]{0:T(128)S(1)} %pad_add_fusion.where_ref, f32[16,8,256]{2,1,0:T(8,128)S(1)} %all_to_all.15.mean_ref), custom_call_target="tpu_custom_call" | custom-call | tf_op jit(solution)/shard_map/factor/pallas_call | solution.py:287
  110.3 18.1 %all_to_all.16.got_ref = f32[32,8,384]{2,1,0:T(8,128)S(1)} all-to-all(f32[32,8,384]{2,1,0:T(8,128)S(1)} %factor.1), channel_id=1, replica_groups=mesh['fsdp'=16,'dp'=32] {'dp'}, dimensions={0} | all-to-all | bytes 786432 | tf_op jit(solution)/shard_map/all_to_all | solution.py:295
  128.4 1.8 %unpack.1 = (f32[4,14336]{1,0:T(4,128)}, f32[4,448]{1,0:T(4,128)}, f32[32,896]{1,0:T(8,128)}) custom-call(s32[4]{0:T(128)S(1)} %pad_add_fusion.where_ref, f32[32,8,384]{2,1,0:T(8,128)S(1)} %all_to_all.16.got_ref, f32[4,7168]{1,0:T(4,128)S(1)} %get-tuple-element.34.kept_ref, f32[4,7168]{1,0:T(4,128)S(1)} %collective-permute-done.9.got_row_ref), custom_call_target="tpu_custom_call" | custom-call | tf_op jit(solution)/shard_map/unpack/pallas_call | solution.py:296
  (42 shorter events, 7.0 us)
Async XLA Ops:
  0.6 0.7 copy-start
  2.7 2.0 %copy-start.1 = (bf16[1,128,14336]{2,1,0:T(8,128)(2,1)S(1)}, bf16[1,128,14336]{2,1,0:T(8,128)(2,1)}, u32[]{:S(2)}) copy-start(bf16[1,128,14336]{2,1,0:T(8,128)(2,1)} %param.7) | copy-start | bytes 11010052
  4.8 12.3 %copy-start.2 = (bf16[1,128,14336]{2,1,0:T(8,128)(2,1)S(1)}, bf16[1,128,14336]{2,1,0:T(8,128)(2,1)}, u32[]{:S(2)}) copy-start(bf16[1,128,14336]{2,1,0:T(8,128)(2,1)} %param.7) | copy-start | bytes 11010052
  6.0 13.3 %copy-start.3 = (f32[896,32]{0,1:T(8,128)S(1)}, f32[896,32]{0,1:T(8,128)}, u32[]{:S(2)}) copy-start(f32[896,32]{0,1:T(8,128)} %param.9) | copy-start | bytes 344068
  6.0 12.3 %collective-permute-start = (f32[32,7168]{1,0:T(8,128)S(1)}, f32[32,7168]{1,0:T(8,128)S(1)}, u32[]{:S(2)}, u32[]{:S(2)}) collective-permute-start(f32[32,7168]{1,0:T(8,128)S(1)} %get-tuple-element.22), channel_id=1, source_target_pairs={{0,32},{32,0},{64,96},{96,64},{128,160},{160,128},{192,224},{224,1... | collective-permute-start | bytes 2752520 | tf_op jit(solution)/shard_map/ppermute | solution.py:240
  15.0 4.4 %collective-permute-start.5 = (f32[32,7168]{1,0:T(8,128)S(1)}, f32[32,7168]{1,0:T(8,128)S(1)}, u32[]{:S(2)}, u32[]{:S(2)}) collective-permute-start(f32[32,7168]{1,0:T(8,128)S(1)} %get-tuple-element.27), channel_id=1, source_target_pairs={{0,32},{32,0},{64,96},{96,64},{128,160},{160,128},{192,224},{224,1... | collective-permute-start | bytes 2752520 | tf_op jit(solution)/shard_map/ppermute | solution.py:241
  19.4 10.6 %collective-permute-start.1 = (f32[8,10752]{1,0:T(8,128)S(1)}, f32[8,10752]{1,0:T(8,128)S(1)}, u32[]{:S(2)}, u32[]{:S(2)}) collective-permute-start(f32[8,10752]{1,0:T(8,128)S(1)} %get-tuple-element.46), channel_id=1, source_target_pairs={{0,448},{64,0},{128,64},{192,128},{256,192},{320,256},{384,320},{4... | collective-permute-start | bytes 1032200 | tf_op jit(solution)/shard_map/ppermute | solution.py:248
  21.3 10.7 %collective-permute-start.6 = (f32[8,10752]{1,0:T(8,128)S(1)}, f32[8,10752]{1,0:T(8,128)S(1)}, u32[]{:S(2)}, u32[]{:S(2)}) collective-permute-start(f32[8,10752]{1,0:T(8,128)S(1)} %get-tuple-element.45), channel_id=1, source_target_pairs={{448,0},{0,64},{64,128},{128,192},{192,256},{256,320},{320,384},{3... | collective-permute-start | bytes 1032200 | tf_op jit(solution)/shard_map/ppermute | solution.py:267
  30.1 9.6 %collective-permute-start.2 = (f32[8,10752]{1,0:T(8,128)S(1)}, f32[8,10752]{1,0:T(8,128)S(1)}, u32[]{:S(2)}, u32[]{:S(2)}) collective-permute-start(f32[8,10752]{1,0:T(8,128)S(1)} %pad_maximum_fusion.2), channel_id=1, source_target_pairs={{0,448},{64,0},{128,64},{192,128},{256,192},{320,256},{384,320},{4... | collective-permute-start | bytes 1032200 | tf_op jit(solution)/shard_map/ppermute | solution.py:262
  32.1 18.9 %copy-start.4 = (s32[32]{0:T(128)S(1)}, s32[32]{0:T(128)}, u32[]{:S(2)}) copy-start(s32[32]{0:T(128)} %param.10) | copy-start | bytes 388
  32.1 18.9 %copy-start.5 = (s32[32]{0:T(128)S(1)}, s32[32]{0:T(128)}, u32[]{:S(2)}) copy-start(s32[32]{0:T(128)} %param.11) | copy-start | bytes 388
  32.2 11.1 %collective-permute-start.7 = (f32[8,10752]{1,0:T(8,128)S(1)}, f32[8,10752]{1,0:T(8,128)S(1)}, u32[]{:S(2)}, u32[]{:S(2)}) collective-permute-start(f32[8,10752]{1,0:T(8,128)S(1)} %pad_maximum_fusion.4), channel_id=1, source_target_pairs={{448,0},{0,64},{64,128},{128,192},{192,256},{256,320},{320,384},{3... | collective-permute-start | bytes 1032200 | tf_op jit(solution)/shard_map/ppermute | solution.py:267
  39.8 9.2 %collective-permute-start.3 = (f32[8,10752]{1,0:T(8,128)S(1)}, f32[8,10752]{1,0:T(8,128)S(1)}, u32[]{:S(2)}, u32[]{:S(2)}) collective-permute-start(f32[8,10752]{1,0:T(8,128)S(1)} %pad_maximum_fusion.3), channel_id=1, source_target_pairs={{0,448},{64,0},{128,64},{192,128},{256,192},{320,256},{384,320},{4... | collective-permute-start | bytes 1032200 | tf_op jit(solution)/shard_map/ppermute | solution.py:262
  43.4 11.5 %collective-permute-start.8 = (f32[8,10752]{1,0:T(8,128)S(1)}, f32[8,10752]{1,0:T(8,128)S(1)}, u32[]{:S(2)}, u32[]{:S(2)}) collective-permute-start(f32[8,10752]{1,0:T(8,128)S(1)} %pad_maximum_fusion.5), channel_id=1, source_target_pairs={{448,0},{0,64},{64,128},{128,192},{192,256},{256,320},{320,384},{3... | collective-permute-start | bytes 1032200 | tf_op jit(solution)/shard_map/ppermute | solution.py:267
  49.1 9.8 %collective-permute-start.4 = (f32[8,10752]{1,0:T(8,128)S(1)}, f32[8,10752]{1,0:T(8,128)S(1)}, u32[]{:S(2)}, u32[]{:S(2)}) collective-permute-start(f32[8,10752]{1,0:T(8,128)S(1)} %step.1), channel_id=1, source_target_pairs={{0,448},{64,0},{128,64},{192,128},{256,192},{320,256},{384,320},{4... | collective-permute-start | bytes 1032200 | tf_op jit(solution)/shard_map/ppermute | solution.py:262
  61.3 22.6 %all-to-all-start = ((f32[32,8,256]{2,1,0:T(8,128)}), f32[32,8,256]{2,1,0:T(8,128)S(1)}, u32[]{:S(2)}, u32[]{:S(2)}) async-start(f32[32,8,256]{2,1,0:T(8,128)} %get-tuple-element.31), calls=%async_computation | async-start | bytes 524288 | tf_op jit(solution)/shard_map/all_to_all | solution.py:284
  73.5 10.5 %collective-permute-start.9 = (f32[4,7168]{1,0:T(4,128)S(1)}, f32[4,7168]{1,0:T(4,128)S(1)}, u32[]{:S(2)}, u32[]{:S(2)}) collective-permute-start(f32[4,7168]{1,0:T(4,128)S(1)} %get-tuple-element.32), channel_id=1, source_target_pairs={{0,32},{32,0},{64,96},{96,64},{128,160},{160,128},{192,224},{224,1... | collective-permute-start | bytes 344072 | tf_op jit(solution)/shard_map/ppermute | solution.py:283
